TPU v7x, 32 devices: a whole 2x2x4 slice. The times are simulated.
32 devices in a mesh: dp: 4 (over y, x), expert: 8 (over z, core).
Axes of the slice: x: 2, y: 2, z: 4, core: 2. Of those that a mesh axis runs over, the one named last changes fastest.
Arguments:
- tokens: bfloat16 [25216, 768], P(('dp', 'expert')), may hold values from -6 to 6
- image_count: int32 [32], P(('dp', 'expert')), may hold values from 1 to 4, as said below
- routes: int32 [25216, 2], P(('dp', 'expert')), may hold values from 0 to 7, all different within a row; in each aligned block of 788 rows (0 to 787, 788 to 1575, ...) at most 246 rows name the same one
- capacity: int32 [8], replicated, may hold values from 123 to 246, as said below
- ln1_gain: bfloat16 [768], P(('dp', 'expert')), may hold values from 0.5 to 1.5
- ln1_bias: bfloat16 [768], P(('dp', 'expert')), may hold values from -0.625 to 0.625
- qkv_weight: bfloat16 [768, 2304], P(('dp', 'expert')), may hold values from -0.21875 to 0.21875
- qv_bias: bfloat16 [2, 768], P(None, ('dp', 'expert')), may hold values from -0.625 to 0.625
- out_weight: bfloat16 [768, 768], P(('dp', 'expert')), may hold values from -0.875 to 0.875
- out_bias: bfloat16 [768], P(('dp', 'expert')), may hold values from -0.625 to 0.625
- ln2_gain: bfloat16 [768], P(('dp', 'expert')), may hold values from 0.5 to 1.5
- ln2_bias: bfloat16 [768], P(('dp', 'expert')), may hold values from -0.625 to 0.625
- router_weight: bfloat16 [768, 8], P(('dp', 'expert')), may hold values from -0.15625 to 0.15625
- expert_in: bfloat16 [8, 768, 3072], P('expert', None, 'dp'), may hold values from -0.21875 to 0.21875
- expert_in_bias: bfloat16 [8, 3072], P('expert', 'dp'), may hold values from -0.625 to 0.625
- expert_out: bfloat16 [8, 3072, 768], P('expert', 'dp'), may hold values from -0.4375 to 0.4375
- expert_out_bias: bfloat16 [8, 768], P('expert', 'dp'), may hold values from -1.5 to 1.5
- cotangent: bfloat16 [25216, 768], P(('dp', 'expert')), may hold values from -6 to 6
Outputs:
- block_out: bfloat16 [25216, 768], P(('dp', 'expert'))
- tokens_grad: float32 [25216, 768], P(('dp', 'expert'))
- ln1_gain_grad: float32 [768], P(('dp', 'expert'))
- ln1_bias_grad: float32 [768], P(('dp', 'expert'))
- qkv_weight_grad: float32 [768, 2304], P(('dp', 'expert'))
- qv_bias_grad: float32 [2, 768], P(None, ('dp', 'expert'))
- out_weight_grad: float32 [768, 768], P(('dp', 'expert'))
- out_bias_grad: float32 [768], P(('dp', 'expert'))
- ln2_gain_grad: float32 [768], P(('dp', 'expert'))
- ln2_bias_grad: float32 [768], P(('dp', 'expert'))
- router_weight_grad: float32 [768, 8], P(('dp', 'expert'))
- expert_in_grad: float32 [8, 768, 3072], P('expert', None, 'dp')
- expert_in_bias_grad: float32 [8, 3072], P('expert', 'dp')
- expert_out_grad: float32 [8, 3072, 768], P('expert', 'dp')
- expert_out_bias_grad: float32 [8, 768], P('expert', 'dp')
Inputs may be any that keep to these rules, and one draw needn't show every extreme that they name: `routes`: within the rows of one device, each expert is named by at most 246 rows, and one expert by exactly 246 rows in some devices. Some expert's capacity is exactly 246. A device holds images in its first image_count slots; the rows of the other slots take no expert slot. Some device holds 4 images.
All inputs are finite; a program needn't handle non-finite values.
Results may differ from a plain program's by a relative error of at most 0.014.
Values may be sent and summed in bfloat16 or wider, within the bound.
No kernel may reach another device: no remote copies, remote signals or barrier semaphores. Data moves between devices by JAX's collectives and lax.ppermute only.
A program may use at most 256 MiB of HBM per device.

v0:
```python
import math

import jax
import jax.numpy as jnp
from jax import lax
from jax.sharding import PartitionSpec as P

HEADS = 12
SEQ = 197


EPS_NORM = 1e-06
NEG_FILL = -1e30


def norm_layer(values, norm_gain, norm_bias):
    centered = values - jnp.mean(values, axis=-1, keepdims=True)
    variance = jnp.mean(centered * centered, axis=-1, keepdims=True)
    return centered * lax.rsqrt(variance + EPS_NORM) * norm_gain + norm_bias


def gelu_piece(pre_act):
    return jax.nn.gelu(pre_act, approximate=True)


def contract_rows(left, right):
    return lax.dot_general(
        left, right, (((0,), (0,)), ((), ())), preferred_element_type=jnp.float32
    )


def contract_cols(left, right):
    return lax.dot_general(
        left, right, (((1,), (1,)), ((), ())), preferred_element_type=jnp.float32
    )


def route_slots(routes_block, alive_block, capacity, slot_cap):
    expert_count = capacity.shape[0]
    expert_ids = jnp.arange(expert_count, dtype=jnp.int32)
    first_hit = ((routes_block[:, 0:1] == expert_ids[None, :]) & alive_block[:, None]).astype(
        jnp.int32
    )
    second_hit = ((routes_block[:, 1:2] == expert_ids[None, :]) & alive_block[:, None]).astype(
        jnp.int32
    )
    ahead_first = jnp.cumsum(first_hit, axis=0) - first_hit
    ahead_second = (
        jnp.cumsum(second_hit, axis=0) - second_hit + jnp.sum(first_hit, axis=0, keepdims=True)
    )
    place_first = jnp.sum(first_hit * ahead_first, axis=1)
    place_second = jnp.sum(second_hit * ahead_second, axis=1)
    limit_first = jnp.sum(first_hit * capacity[None, :], axis=1)
    limit_second = jnp.sum(second_hit * capacity[None, :], axis=1)
    keep_first = place_first < limit_first
    keep_second = place_second < limit_second
    dump_slot = expert_count * slot_cap
    slot_first = jnp.where(keep_first, routes_block[:, 0] * slot_cap + place_first, dump_slot)
    slot_second = jnp.where(keep_second, routes_block[:, 1] * slot_cap + place_second, dump_slot)
    return (slot_first, slot_second, keep_first, keep_second)


def split_heads(qkv_rows, head_count):
    token_count = qkv_rows.shape[0]
    model_width = qkv_rows.shape[1] // 3
    shaped = qkv_rows.reshape(token_count, 3, head_count, model_width // head_count)
    return (shaped[:, 0], shaped[:, 1], shaped[:, 2])


def attention_scores(query, keyed, same_image):
    scale = 1.0 / math.sqrt(query.shape[-1])
    scores = jnp.einsum("qhd,khd->hqk", query, keyed, preferred_element_type=jnp.float32) * scale
    return jnp.where(same_image[None], scores, NEG_FILL)


def attention_forward(qkv_rows, same_image, head_count):
    query, keyed, valued = split_heads(qkv_rows, head_count)
    scores = attention_scores(query, keyed, same_image)
    row_max = jnp.max(scores, axis=-1, keepdims=True)
    exponent = jnp.exp(scores - row_max)
    row_total = jnp.sum(exponent, axis=-1, keepdims=True)
    probabilities = (exponent / row_total).astype(jnp.bfloat16)
    attended = jnp.einsum("hqk,khd->qhd", probabilities, valued, preferred_element_type=jnp.float32)
    return (
        attended.reshape(qkv_rows.shape[0], -1).astype(jnp.bfloat16),
        row_max + jnp.log(row_total),
    )


def attention_backward(qkv_rows, same_image, log_total, attended_grad, head_count):
    query, keyed, valued = split_heads(qkv_rows, head_count)
    scale = 1.0 / math.sqrt(query.shape[-1])
    probabilities = jnp.exp(attention_scores(query, keyed, same_image) - log_total)
    out_grad = attended_grad.reshape(query.shape)
    value_grad = jnp.einsum(
        "hqk,qhd->khd",
        probabilities.astype(jnp.bfloat16),
        out_grad,
        preferred_element_type=jnp.float32,
    )
    prob_grad = jnp.einsum("qhd,khd->hqk", out_grad, valued, preferred_element_type=jnp.float32)
    row_inner = jnp.sum(probabilities * prob_grad, axis=-1, keepdims=True)
    score_grad = (probabilities * (prob_grad - row_inner)).astype(jnp.bfloat16)
    query_grad = (
        jnp.einsum("hqk,khd->qhd", score_grad, keyed, preferred_element_type=jnp.float32) * scale
    )
    key_grad = (
        jnp.einsum("hqk,qhd->khd", score_grad, query, preferred_element_type=jnp.float32) * scale
    )
    return jnp.stack([query_grad, key_grad, value_grad], axis=1).reshape(qkv_rows.shape[0], -1)


def local(
    tokens,
    image_count,
    routes,
    capacity,
    ln1_gain,
    ln1_bias,
    qkv_weight,
    qv_bias,
    out_weight,
    out_bias,
    ln2_gain,
    ln2_bias,
    router_weight,
    expert_in,
    expert_in_bias,
    expert_out,
    expert_out_bias,
    cotangent,
):
    dense = (
        lax.all_gather(ln1_gain, ("dp", "expert"), axis=0, tiled=True),
        lax.all_gather(ln1_bias, ("dp", "expert"), axis=0, tiled=True),
        lax.all_gather(qkv_weight, ("dp", "expert"), axis=0, tiled=True),
        lax.all_gather(qv_bias, ("dp", "expert"), axis=1, tiled=True),
        lax.all_gather(out_weight, ("dp", "expert"), axis=0, tiled=True),
        lax.all_gather(out_bias, ("dp", "expert"), axis=0, tiled=True),
        lax.all_gather(ln2_gain, ("dp", "expert"), axis=0, tiled=True),
        lax.all_gather(ln2_bias, ("dp", "expert"), axis=0, tiled=True),
        lax.all_gather(router_weight, ("dp", "expert"), axis=0, tiled=True),
    )
    expert_set = (
        lax.all_gather(expert_in, "dp", axis=2, tiled=True),
        lax.all_gather(expert_in_bias, "dp", axis=1, tiled=True),
        lax.all_gather(expert_out, "dp", axis=1, tiled=True),
        lax.all_gather(expert_out_bias, "dp", axis=1, tiled=True),
    )
    token_count, model_width = tokens.shape
    expert_count = capacity.shape[0]
    slot_cap = max(2, 5 * token_count // (2 * expert_count))
    row_index = jnp.arange(token_count, dtype=jnp.int32)
    image_index = row_index // SEQ
    alive_rows = image_index < image_count[0]
    alive_f = alive_rows.astype(jnp.float32)[:, None]
    same_image = image_index[:, None] == image_index[None, :]
    tokens_f = tokens.astype(jnp.float32)
    gain_one = dense[0].astype(jnp.float32)
    bias_one = dense[1].astype(jnp.float32)
    gain_two = dense[6].astype(jnp.float32)
    bias_two = dense[7].astype(jnp.float32)
    normed_one = norm_layer(tokens_f, gain_one, bias_one).astype(jnp.bfloat16)
    qv_pair = dense[3].astype(jnp.float32)
    bias_full = jnp.concatenate([qv_pair[0], jnp.zeros((model_width,), jnp.float32), qv_pair[1]])
    qkv_rows = (
        jnp.dot(normed_one, dense[2], preferred_element_type=jnp.float32) + bias_full
    ).astype(jnp.bfloat16)
    attended, log_total = attention_forward(qkv_rows, same_image, HEADS)
    attn_out = jnp.dot(attended, dense[4], preferred_element_type=jnp.float32) + dense[5].astype(
        jnp.float32
    )
    after_attn = tokens_f + alive_f * attn_out
    normed_two = norm_layer(after_attn, gain_two, bias_two).astype(jnp.bfloat16)
    logits = jnp.dot(normed_two, dense[8], preferred_element_type=jnp.float32)
    gate_probs = jax.nn.softmax(logits, axis=-1)
    slot_first, slot_second, keep_first, keep_second = route_slots(
        routes, alive_rows, capacity, slot_cap
    )
    expert_ids = jnp.arange(expert_count, dtype=jnp.int32)
    first_hit = routes[:, 0:1] == expert_ids[None, :]
    second_hit = routes[:, 1:2] == expert_ids[None, :]
    gate_first = jnp.sum(jnp.where(first_hit, gate_probs, 0.0), axis=1) * keep_first.astype(
        jnp.float32
    )
    gate_second = jnp.sum(jnp.where(second_hit, gate_probs, 0.0), axis=1) * keep_second.astype(
        jnp.float32
    )
    outgoing = jnp.zeros((expert_count * slot_cap + 1, model_width), jnp.bfloat16)
    outgoing = outgoing.at[slot_first].add(normed_two).at[slot_second].add(normed_two)[:-1]
    incoming = lax.all_to_all(
        outgoing.reshape(expert_count, slot_cap, model_width),
        "expert",
        split_axis=0,
        concat_axis=0,
        tiled=True,
    )
    slot_rows = incoming.reshape(-1, model_width)
    w_in = expert_set[0][0]
    b_in = expert_set[1][0].astype(jnp.float32)
    w_out = expert_set[2][0]
    b_out = expert_set[3][0].astype(jnp.float32)
    pre_act = jnp.dot(slot_rows, w_in, preferred_element_type=jnp.float32) + b_in
    activated = gelu_piece(pre_act).astype(jnp.bfloat16)
    expert_rows = (jnp.dot(activated, w_out, preferred_element_type=jnp.float32) + b_out).astype(
        jnp.bfloat16
    )
    returned = lax.all_to_all(
        expert_rows.reshape(incoming.shape), "expert", split_axis=0, concat_axis=0, tiled=True
    )
    returned_flat = jnp.concatenate(
        [returned.reshape(-1, model_width), jnp.zeros((1, model_width), jnp.bfloat16)], axis=0
    )
    picked_first = returned_flat[slot_first].astype(jnp.float32)
    picked_second = returned_flat[slot_second].astype(jnp.float32)
    moe_out = gate_first[:, None] * picked_first + gate_second[:, None] * picked_second
    block_value = after_attn + alive_f * moe_out
    dense_back = (
        lax.all_gather(ln1_gain, ("dp", "expert"), axis=0, tiled=True),
        lax.all_gather(ln1_bias, ("dp", "expert"), axis=0, tiled=True),
        lax.all_gather(qkv_weight, ("dp", "expert"), axis=0, tiled=True),
        lax.all_gather(qv_bias, ("dp", "expert"), axis=1, tiled=True),
        lax.all_gather(out_weight, ("dp", "expert"), axis=0, tiled=True),
        lax.all_gather(out_bias, ("dp", "expert"), axis=0, tiled=True),
        lax.all_gather(ln2_gain, ("dp", "expert"), axis=0, tiled=True),
        lax.all_gather(ln2_bias, ("dp", "expert"), axis=0, tiled=True),
        lax.all_gather(router_weight, ("dp", "expert"), axis=0, tiled=True),
    )
    upstream = cotangent.astype(jnp.float32)
    moe_grad = alive_f * upstream
    gate_grad_first = jnp.sum(moe_grad * picked_first, axis=1) * keep_first.astype(jnp.float32)
    gate_grad_second = jnp.sum(moe_grad * picked_second, axis=1) * keep_second.astype(jnp.float32)
    slot_grad = jnp.zeros((expert_count * slot_cap + 1, model_width), jnp.float32)
    slot_grad = (
        slot_grad.at[slot_first]
        .add(gate_first[:, None] * moe_grad)
        .at[slot_second]
        .add(gate_second[:, None] * moe_grad)[:-1]
    )
    slot_grad = slot_grad.astype(jnp.bfloat16).reshape(expert_count, slot_cap, model_width)
    rows_grad = lax.all_to_all(
        slot_grad, "expert", split_axis=0, concat_axis=0, tiled=True
    ).reshape(-1, model_width)
    expert_back = (
        lax.all_gather(expert_in, "dp", axis=2, tiled=True),
        lax.all_gather(expert_in_bias, "dp", axis=1, tiled=True),
        lax.all_gather(expert_out, "dp", axis=1, tiled=True),
        lax.all_gather(expert_out_bias, "dp", axis=1, tiled=True),
    )
    w_in_back = expert_back[0][0]
    w_out_back = expert_back[2][0]
    w_out_grad = contract_rows(activated, rows_grad)
    b_out_grad = jnp.sum(rows_grad, axis=0, dtype=jnp.float32)
    act_grad = contract_cols(rows_grad, w_out_back)
    gelu_value, gelu_pull = jax.vjp(gelu_piece, pre_act)
    pre_grad = gelu_pull(act_grad)[0].astype(jnp.bfloat16)
    w_in_grad = contract_rows(slot_rows, pre_grad)
    b_in_grad = jnp.sum(pre_grad, axis=0, dtype=jnp.float32)
    buffer_grad = contract_cols(pre_grad, w_in_back).astype(jnp.bfloat16)
    expert_grads = (
        lax.psum_scatter(
            w_in_grad[None].astype(jnp.bfloat16), "dp", scatter_dimension=2, tiled=True
        ).astype(jnp.float32),
        lax.psum_scatter(
            b_in_grad[None].astype(jnp.bfloat16), "dp", scatter_dimension=1, tiled=True
        ).astype(jnp.float32),
        lax.psum_scatter(
            w_out_grad[None].astype(jnp.bfloat16), "dp", scatter_dimension=1, tiled=True
        ).astype(jnp.float32),
        lax.psum_scatter(
            b_out_grad[None].astype(jnp.bfloat16), "dp", scatter_dimension=1, tiled=True
        ).astype(jnp.float32),
    )
    buffer_back = lax.all_to_all(
        buffer_grad.reshape(incoming.shape), "expert", split_axis=0, concat_axis=0, tiled=True
    )
    buffer_flat = jnp.concatenate(
        [buffer_back.reshape(-1, model_width), jnp.zeros((1, model_width), jnp.bfloat16)], axis=0
    )
    expert_part = buffer_flat[slot_first].astype(jnp.float32) + buffer_flat[slot_second].astype(
        jnp.float32
    )
    placed_grad = jnp.where(first_hit, gate_grad_first[:, None], 0.0) + jnp.where(
        second_hit, gate_grad_second[:, None], 0.0
    )
    logit_grad = (
        gate_probs * (placed_grad - jnp.sum(gate_probs * placed_grad, axis=-1, keepdims=True))
    ).astype(jnp.bfloat16)
    router_grad = contract_rows(normed_two, logit_grad)
    normed_two_grad = contract_cols(logit_grad, dense_back[8]) + expert_part
    norm_two_value, norm_two_pull = jax.vjp(norm_layer, after_attn, gain_two, bias_two)
    after_ln_grad, gain_two_grad, bias_two_grad = norm_two_pull(normed_two_grad)
    after_grad = upstream + after_ln_grad
    attn_grad = (alive_f * after_grad).astype(jnp.bfloat16)
    out_weight_grad = contract_rows(attended, attn_grad)
    out_bias_grad = jnp.sum(attn_grad, axis=0, dtype=jnp.float32)
    attended_grad = contract_cols(attn_grad, dense_back[4]).astype(jnp.bfloat16)
    qkv_grad = attention_backward(qkv_rows, same_image, log_total, attended_grad, HEADS).astype(
        jnp.bfloat16
    )
    qkv_weight_grad = contract_rows(normed_one, qkv_grad)
    qkv_sums = jnp.sum(qkv_grad, axis=0, dtype=jnp.float32)
    qv_bias_grad = jnp.stack([qkv_sums[:model_width], qkv_sums[2 * model_width :]], axis=0)
    normed_one_grad = contract_cols(qkv_grad, dense_back[2])
    norm_one_value, norm_one_pull = jax.vjp(norm_layer, tokens_f, gain_one, bias_one)
    input_ln_grad, gain_one_grad, bias_one_grad = norm_one_pull(normed_one_grad)
    tokens_grad = after_grad + input_ln_grad
    dense_grads = (
        lax.psum_scatter(gain_one_grad, ("dp", "expert"), scatter_dimension=0, tiled=True),
        lax.psum_scatter(bias_one_grad, ("dp", "expert"), scatter_dimension=0, tiled=True),
        lax.psum_scatter(qkv_weight_grad, ("dp", "expert"), scatter_dimension=0, tiled=True),
        lax.psum_scatter(qv_bias_grad, ("dp", "expert"), scatter_dimension=1, tiled=True),
        lax.psum_scatter(out_weight_grad, ("dp", "expert"), scatter_dimension=0, tiled=True),
        lax.psum_scatter(out_bias_grad, ("dp", "expert"), scatter_dimension=0, tiled=True),
        lax.psum_scatter(gain_two_grad, ("dp", "expert"), scatter_dimension=0, tiled=True),
        lax.psum_scatter(bias_two_grad, ("dp", "expert"), scatter_dimension=0, tiled=True),
        lax.psum_scatter(router_grad, ("dp", "expert"), scatter_dimension=0, tiled=True),
    )
    return (
        block_value.astype(jnp.bfloat16),
        tokens_grad,
        dense_grads[0],
        dense_grads[1],
        dense_grads[2],
        dense_grads[3],
        dense_grads[4],
        dense_grads[5],
        dense_grads[6],
        dense_grads[7],
        dense_grads[8],
        expert_grads[0],
        expert_grads[1],
        expert_grads[2],
        expert_grads[3],
    )


def solution(mesh):
    return jax.shard_map(
        local,
        mesh=mesh,
        in_specs=(
            P(("dp", "expert"), None),
            P(("dp", "expert")),
            P(("dp", "expert"), None),
            P(),
            P(("dp", "expert")),
            P(("dp", "expert")),
            P(("dp", "expert"), None),
            P(None, ("dp", "expert")),
            P(("dp", "expert"), None),
            P(("dp", "expert")),
            P(("dp", "expert")),
            P(("dp", "expert")),
            P(("dp", "expert"), None),
            P("expert", None, "dp"),
            P("expert", "dp"),
            P("expert", "dp", None),
            P("expert", "dp"),
            P(("dp", "expert"), None),
        ),
        out_specs=(
            P(("dp", "expert"), None),
            P(("dp", "expert"), None),
            P(("dp", "expert")),
            P(("dp", "expert")),
            P(("dp", "expert"), None),
            P(None, ("dp", "expert")),
            P(("dp", "expert"), None),
            P(("dp", "expert")),
            P(("dp", "expert")),
            P(("dp", "expert")),
            P(("dp", "expert"), None),
            P("expert", None, "dp"),
            P("expert", "dp"),
            P("expert", "dp", None),
            P("expert", "dp"),
        ),
        check_vma=False,
    )
```

profile of v0, /device:TPU:0, one launch (start us, length us, event | category | flops | bytes accessed | tf_op | source)
XLA Modules:
  0.0 1032.5 jit_solution(2514252997019987375)
XLA Ops:
  14.3 42.3 %all-reduce.18 = (bf16[768]{0:T(1024)(128)(2,1)S(1)}, bf16[768]{0:T(1024)(128)(2,1)S(1)}, bf16[768]{0:T(1024)(128)(2,1)S(1)}, bf16[768]{0:T(1024)(128)(2,1)S(1)}, bf16[768]{0:T(1024)(128)(2,1)S(1)}) all-reduce(bf16[768]{0:T(1024)(128)(2,1)S(1)} %dynamic-update-slice.1, ...), channel_id=1, replica_groups=mesh['dp'=4,'expert'=8] {'dp','expert'}, use_global_device_ids=true, to_apply=%add.5 | all-reduce | flops 3840 | bytes 15360
  59.4 40.8 %all-gather = bf16[32,24,2]{1,2,0:T(2,128)(2,1)S(1)} all-gather(bf16[1,24,2]{1,2,0:T(2,128)(2,1)S(1)} %bitcast.147), channel_id=1, replica_groups=mesh['dp'=4,'expert'=8] {'dp','expert'}, dimensions={0}, use_global_device_ids=true | all-gather | bytes 3168 | tf_op jit(solution)/shard_map/all_gather | solution.py:137
  100.6 2.0 reduce-window.16
  106.5 6.9 add_convert_fusion
  113.4 6.2 copy.72
  119.7 19.4 %fusion.13 = (f32[12,788]{1,0:T(8,128)S(1)}, f32[12,788,788]{1,2,0:T(8,128)}) fusion(pred[788,788]{0,1:T(8,128)(4,1)S(1)} %broadcast_compare_fusion, bf16[788,3,12,64]{0,3,2,1:T(8,128)(2,1)} %bitcast.128), kind=kOutput, calls=%fused_computation.29 | convolution fusion | flops 976114496 | bytes 33216592 | tf_op jit(solution)/shard_map/qhd,khd->hqk/dot_general | solution.py:72
  139.1 15.6 %fusion = f32[12,788]{1,0:T(8,128)S(1)} fusion(f32[12,788]{1,0:T(8,128)S(1)} %get-tuple-element.65, f32[12,788,788]{1,2,0:T(8,128)} %get-tuple-element.66, pred[788,788]{0,1:T(8,128)(4,1)S(1)} %broadcast_compare_fusion), kind=kLoop, calls=%fused_computation.16 | loop fusion | flops 29795856 | bytes 30501904 | tf_op jit(solution)/shard_map/reduce_sum | solution.py:81
  155.3 17.9 %fusion.60 = bf16[12,64,788]{2,1,0:T(8,128)(2,1)} fusion(f32[12,788]{1,0:T(8,128)S(1)} %fusion, f32[12,788]{1,0:T(8,128)S(1)} %get-tuple-element.65, f32[12,788,788]{1,2,0:T(8,128)} %get-tuple-element.66, pred[788,788]{0,1:T(8,128)(4,1)S(1)} %broadcast_compare_fusion, bf16[788,3,12,64]{0,3,2,1:T(8,128)(2,1)} %bitcast.129), kind=kOutput, calls=%fused_computation.92 | convolution fusion | flops 991631808 | bytes 37345552 | tf_op jit(solution)/shard_map/hqk,khd->qhd/dot_general | solution.py:83
  173.2 3.4 fusion.99
  177.1 10.7 %scatter_custom_fusion = bf16[1969,768]{1,0:T(8,128)(2,1)} fusion(s32[788]{0:T(1024)S(1)} %get-tuple-element.28, bf16[]{:T(256)} %constant.65.clone.1, f32[788,768]{1,0:T(8,128)S(1)} %get-tuple-element.68, f32[768]{0:T(1024)S(1)} %convert_element_type.190, f32[768]{0:T(1024)S(1)} %convert_element_type.189, f32[788]{0:T(1024)S(1)} %fusion.84, ...), kind=kCustom, calls=%fused_computation.94 | custom fusion | flops 3631104 | bytes 5473794 | tf_op jit(solution)/shard_map/scatter-add | solution.py:190
  187.9 12.2 %scatter_custom_fusion.1 = bf16[1969,768]{1,0:T(8,128)(2,1)} fusion(bf16[1969,768]{1,0:T(8,128)(2,1)} %scatter_custom_fusion, s32[788]{0:T(1024)S(1)} %get-tuple-element.27, f32[788,768]{1,0:T(8,128)S(1)} %get-tuple-element.68, f32[768]{0:T(1024)S(1)} %convert_element_type.190, f32[768]{0:T(1024)S(1)} %convert_element_type.189, f32[788]{0:T(1024)S(1)} %fusion.84, ...), kind=kCustom, calls=%fused_computation.192 | custom fusion | flops 3631104 | bytes 5473792 | tf_op jit(solution)/shard_map/scatter-add | solution.py:190
  200.1 3.7 slice.95
  203.7 3.5 reshape.308
  207.2 4.6 all-to-all-start
  214.0 7.7 all-reduce.9
  221.6 8.8 all_gather.54
  230.5 50.8 %all-to-all-done = bf16[8,246,768]{2,1,0:T(8,128)(2,1)} async-done(((bf16[8,246,768]{2,1,0:T(8,128)(2,1)}), bf16[8,246,768]{2,1,0:T(8,128)(2,1)}, u32[]{:S(2)}, u32[]{:S(2)}) %all-to-all-start) | async-done | bytes 3022880 | tf_op jit(solution)/shard_map/all_to_all | solution.py:191
  281.3 3.4 reshape.309
  284.7 23.8 %multiply_convert_fusion.1 = (bf16[1968,3072]{1,0:T(8,128)(2,1)}, f32[1968,3072]{1,0:T(8,128)}) fusion(f32[3072]{0:T(1024)S(1)} %bitcast.144, bf16[1968,768]{1,0:T(8,128)(2,1)} %reshape.309, bf16[1,768,3072]{2,1,0:T(8,128)(2,1)} %all-gather.11.cloned.1.call-done), kind=kOutput, calls=%fused_computation.25 | convolution fusion | flops 9346646016 | bytes 44027904 | tf_op jit(solution)/shard_map/dot_general | solution.py:203
  308.6 15.0 %add_convert_fusion.1 = bf16[1968,768]{1,0:T(8,128)(2,1)} fusion(bf16[1968,3072]{1,0:T(8,128)(2,1)} %get-tuple-element.69, bf16[1,3072,768]{2,1,0:T(8,128)(2,1)} %all-gather.13.cloned.1.call-done, f32[768]{0:T(1024)S(1)} %add.253), kind=kOutput, calls=%fused_computation.34 | convolution fusion | flops 9289211904 | bytes 19835904 | tf_op jit(solution)/shard_map/dot_general | solution.py:205
  323.5 3.5 reshape.310
  327.0 4.6 all-to-all-start.1
  331.7 98.6 %all-gather.1 = bf16[32,24,8]{1,2,0:T(8,128)(2,1)S(1)} all-gather(bf16[1,24,8]{1,2,0:T(8,128)(2,1)S(1)} %bitcast.146), channel_id=1, replica_groups=mesh['dp'=4,'expert'=8] {'dp','expert'}, dimensions={0}, use_global_device_ids=true | all-gather | bytes 12672 | tf_op jit(solution)/shard_map/all_gather | solution.py:142
  432.5 3.5 reshape.311
  435.9 2.1 concatenate.10
  438.0 4.0 gather_fusion.1
  442.0 4.0 gather_fusion
  446.1 3.1 fusion.50
  449.4 11.1 %scatter_custom_fusion.2 = f32[1969,768]{1,0:T(8,128)} fusion(s32[788]{0:T(1024)S(1)} %get-tuple-element.28, f32[]{:T(128)} %constant.58.clone.1, bf16[788,768]{1,0:T(8,128)(2,1)S(1)} %copy-done.2, f32[788]{0:T(1024)S(1)} %broadcast_select_fusion.3, f32[788]{0:T(1024)S(1)} %fusion.87), kind=kCustom, calls=%fused_computation.65 | custom fusion | flops 2420736 | bytes 7273476 | tf_op jit(solution)/shard_map/scatter-add | solution.py:236
  460.5 13.4 %scatter_custom_fusion.3 = f32[1969,768]{1,0:T(8,128)} fusion(f32[1969,768]{1,0:T(8,128)} %scatter_custom_fusion.2, s32[788]{0:T(1024)S(1)} %get-tuple-element.27, bf16[788,768]{1,0:T(8,128)(2,1)S(1)} %copy-done.2, f32[788]{0:T(1024)S(1)} %broadcast_select_fusion.2, f32[788]{0:T(1024)S(1)} %fusion.87), kind=kCustom, calls=%fused_computation.80 | custom fusion | flops 2420736 | bytes 7273472 | tf_op jit(solution)/shard_map/scatter-add | solution.py:238
  473.9 3.0 slice.123
  476.9 2.0 reshape.312
  478.9 73.0 %all_to_all.20 = bf16[8,246,768]{2,1,0:T(8,128)(2,1)S(1)} all-to-all(bf16[8,246,768]{2,1,0:T(8,128)(2,1)} %reshape.312), channel_id=1, replica_groups=mesh['dp'=4,'expert'=8] {'expert'}, dimensions={0} | all-to-all | bytes 6045696 | tf_op jit(solution)/shard_map/all_to_all | solution.py:241
  553.7 2.0 reshape.313
  555.7 32.0 %fusion.101 = (bf16[3072]{0:T(1024)(128)(2,1)S(1)}, bf16[1968,3072]{1,0:T(8,128)(2,1)}) fusion(f32[1968,3072]{1,0:T(8,128)} %get-tuple-element.70, f32[3072]{0:T(1024)S(1)} %bitcast.145, bf16[1968,768]{1,0:T(8,128)(2,1)} %reshape.313, bf16[1,3072,768]{2,1,0:T(8,128)(2,1)} %all-gather.13.cloned.1.call-done), kind=kOutput, calls=%fused_computation.189 | convolution fusion | flops 9419191296 | bytes 44034048 | tf_op jit(solution)/shard_map/dot_general | solution.py:33
  589.3 14.4 %fusion.24 = bf16[1,3072,768]{2,1,0:T(8,128)(2,1)} fusion(bf16[1968,3072]{1,0:T(8,128)(2,1)} %get-tuple-element.69, bf16[1968,768]{1,0:T(8,128)(2,1)S(1)} %copy-done.14), kind=kOutput, calls=%fused_computation.45 | convolution fusion | flops 9288548352 | bytes 19832832 | tf_op jit(solution)/shard_map/dot_general | solution.py:27
  603.8 13.9 %fusion.32 = bf16[1968,768]{1,0:T(8,128)(2,1)S(1)} fusion(bf16[1968,3072]{1,0:T(8,128)(2,1)} %get-tuple-element.78, bf16[1,768,3072]{2,1,0:T(8,128)(2,1)} %all-gather.11.cloned.1.call-done), kind=kOutput, calls=%fused_computation.56 | convolution fusion | flops 9287700480 | bytes 19832832 | tf_op jit(solution)/shard_map/dot_general | solution.py:33
  617.7 2.0 reshape.314
  619.7 3.8 all-to-all-start.3
  623.6 15.3 %fusion.25 = bf16[1,768,3072]{2,1,0:T(8,128)(2,1)} fusion(bf16[1968,768]{1,0:T(8,128)(2,1)} %reshape.309, bf16[1968,3072]{1,0:T(8,128)(2,1)} %get-tuple-element.78), kind=kOutput, calls=%fused_computation.46 | convolution fusion | flops 9288548352 | bytes 19832832 | tf_op jit(solution)/shard_map/dot_general | solution.py:27
  639.2 53.6 %all-to-all-done.3 = bf16[8,246,768]{2,1,0:T(8,128)(2,1)S(1)} async-done(((bf16[8,246,768]{2,1,0:T(8,128)(2,1)}), bf16[8,246,768]{2,1,0:T(8,128)(2,1)S(1)}, u32[]{:S(2)}, u32[]{:S(2)}) %all-to-all-start.3) | async-done | bytes 3022880 | tf_op jit(solution)/shard_map/all_to_all | solution.py:274
  692.8 2.1 reshape.315
  694.9 2.1 concatenate.11
  697.0 4.0 gather_fusion.3
  701.1 4.0 gather_fusion.2
  705.1 3.9 multiply_reduce_fusion.1
  709.1 2.7 fusion.97
  714.0 2.8 fusion.102
  716.8 3.8 convolution_convert_fusion.2
  722.5 28.6 %multiply_reduce_fusion = (f32[12,788]{1,0:T(8,128)S(1)}, f32[12,788,788]{1,2,0:T(8,128)}) fusion(f32[12,788]{1,0:T(8,128)S(1)} %log_add_fusion, f32[12,788,788]{1,2,0:T(8,128)} %get-tuple-element.66, pred[788,788]{0,1:T(8,128)(4,1)S(1)} %copy-done.5, bf16[788,12,64]{0,2,1:T(8,128)(2,1)S(1)} %bitcast.133, bf16[788,3,12,64]{0,3,2,1:T(8,128)(2,1)} %bitcast.130), kind=kOutput, calls=%fused_computation.11 | convolution fusion | flops 991017152 | bytes 67150864 | tf_op jit(solution)/shard_map/qhd,khd->hqk/dot_general | solution.py:101
  751.1 28.8 %multiply_convert_fusion = bf16[12,788,788]{1,2,0:T(8,128)(2,1)} fusion(f32[12,788,788]{1,2,0:T(8,128)} %get-tuple-element.75, f32[12,788]{1,0:T(8,128)S(1)} %get-tuple-element.74, f32[12,788]{1,0:T(8,128)S(1)} %log_add_fusion, f32[12,788,788]{1,2,0:T(8,128)} %get-tuple-element.66, pred[788,788]{0,1:T(8,128)(4,1)S(1)} %copy-done.5), kind=kLoop, calls=%fused_computation.10 | loop fusion | flops 44707968 | bytes 75209872 | tf_op jit(solution)/shard_map/convert_element_type | solution.py:103
  779.9 12.7 %multiply_bitcast_fusion = bf16[788,1,12,64]{0,3,2,1:T(8,128)(2,1)} fusion(bf16[12,788,788]{1,2,0:T(8,128)(2,1)} %multiply_convert_fusion, bf16[788,3,12,64]{0,3,2,1:T(8,128)(2,1)} %bitcast.131), kind=kOutput, calls=%fused_computation.69 | convolution fusion | flops 954980352 | bytes 19617792 | tf_op jit(solution)/shard_map/hqk,qhd->khd/dot_general | solution.py:108
  792.6 10.6 %multiply_bitcast_fusion.1 = bf16[788,1,12,64]{0,3,2,1:T(8,128)(2,1)} fusion(bf16[12,788,788]{1,2,0:T(8,128)(2,1)} %multiply_convert_fusion, bf16[788,3,12,64]{0,3,2,1:T(8,128)(2,1)} %bitcast.132), kind=kOutput, calls=%fused_computation.70 | convolution fusion | flops 954980352 | bytes 19617792 | tf_op jit(solution)/shard_map/hqk,khd->qhd/dot_general | solution.py:105
  803.2 16.3 %fusion.57 = bf16[788,1,12,64]{0,3,2,1:T(8,128)(2,1)} fusion(bf16[788,12,64]{0,2,1:T(8,128)(2,1)S(1)} %bitcast.134, f32[12,788]{1,0:T(8,128)S(1)} %log_add_fusion, f32[12,788,788]{1,2,0:T(8,128)} %get-tuple-element.66, pred[788,788]{0,1:T(8,128)(4,1)S(1)} %copy-done.5), kind=kOutput, calls=%fused_computation.91 | convolution fusion | flops 983575296 | bytes 32884816 | tf_op jit(solution)/shard_map/hqk,qhd->khd/dot_general | solution.py:95
  819.6 2.7 convert_reduce_fusion
  822.3 2.0 copy-done.13
  824.4 6.8 fusion.92
  836.1 7.1 fusion.96
  846.0 38.1 %all-reduce.17 = (f32[768]{0:T(1024)S(1)}, f32[768]{0:T(1024)S(1)}, f32[2,768]{1,0:T(2,128)S(1)}, f32[768]{0:T(1024)S(1)}, f32[768]{0:T(1024)S(1)}, /*index=5*/f32[768]{0:T(1024)S(1)}, f32[768,8]{0,1:T(8,128)S(1)}) all-reduce(f32[768]{0:T(1024)S(1)} %get-tuple-element.17, ...), channel_id=2, replica_groups=mesh['dp'=4,'expert'=8] {'dp','expert'}, use_global_device_ids=true, to_apply=%region_32.33.clone | all-reduce | flops 11520 | bytes 92160
  888.3 4.0 add_add_fusion.2
  892.3 2.9 convert_element_type.219
  895.1 2.9 convert_element_type.214
  898.0 2.3 reduce-scatter.15.cloned.1.call-done
  900.3 125.2 %reduce-scatter.13.cloned.1.call-done = f32[24,2304]{1,0:T(8,128)} async-done(((f32[768,2304]{1,0:T(8,128)}), f32[24,2304]{1,0:T(8,128)}) %reduce-scatter.13.cloned.1.call-update) | async-done | bytes 221200 | tf_op jit(solution)/shard_map/reduce_scatter | solution.py:311
  (225 shorter events, 37.7 us)
Async XLA Ops:
  7.2 51.1 %copy-start.7 = (bf16[788,768]{1,0:T(8,128)(2,1)S(1)}, bf16[788,768]{1,0:T(8,128)(2,1)}, u32[]{:S(2)}) copy-start(bf16[788,768]{1,0:T(8,128)(2,1)} %param.18) | copy-start | bytes 3631108
  7.2 51.6 %copy-start.41 = (s32[788,2]{0,1:T(2,128)S(1)}, s32[788,2]{0,1:T(2,128)}, u32[]{:S(2)}) copy-start(s32[788,2]{0,1:T(2,128)} %param.20) | copy-start | bytes 18916
  7.2 52.2 %copy-start.48 = (bf16[2,24]{1,0:T(2,128)(2,1)S(1)}, bf16[2,24]{1,0:T(2,128)(2,1)}, u32[]{:S(2)}) copy-start(bf16[2,24]{1,0:T(2,128)(2,1)} %param.25) | copy-start | bytes 292
  7.2 99.3 %all-gather.7.cloned.1.call-start = ((), (), s32[]{:S(2)}) async-start(), calls=%async_computation.10 | async-start | bytes 3649536 | tf_op jit(solution)/shard_map/all_gather | solution.py:136
  7.9 165.3 %all-gather.9.cloned.1.call-start = ((), (), s32[]{:S(2)}) async-start(), calls=%async_computation.11 | async-start | bytes 1216512 | tf_op jit(solution)/shard_map/all_gather | solution.py:138
  8.7 97.4 %copy-start.45 = (s32[8]{0:T(128)S(1)}, s32[8]{0:T(128)}, u32[]{:S(2)}) copy-start(s32[8]{0:T(128)} %param.21) | copy-start | bytes 100
  8.7 276.0 %all-gather.11.cloned.1.call-start = ((), (), s32[]{:S(2)}) async-start(), calls=%async_computation.12 | async-start | bytes 5898240 | tf_op jit(solution)/shard_map/all_gather | solution.py:145
  56.6 56.7 %copy-start.42 = (f32[768]{0:T(1024)}, f32[768]{0:T(1024)S(1)}, u32[]{:S(2)}) copy-start(f32[768]{0:T(1024)S(1)} %convert_element_type.179) | copy-start | bytes 9220
  56.6 56.7 %copy-start.37 = (f32[768]{0:T(1024)}, f32[768]{0:T(1024)S(1)}, u32[]{:S(2)}) copy-start(f32[768]{0:T(1024)S(1)} %convert_element_type.178) | copy-start | bytes 9220
  58.2 55.1 %copy-start.23 = (f32[788]{0:T(1024)}, f32[788]{0:T(1024)S(1)}, u32[]{:S(2)}) copy-start(f32[788]{0:T(1024)S(1)} %broadcast_multiply_fusion.1) | copy-start | bytes 9460
  58.8 0.6 copy-start.25
  58.8 54.5 %copy-start.39 = (f32[788]{0:T(1024)}, f32[788]{0:T(1024)S(1)}, u32[]{:S(2)}) copy-start(f32[788]{0:T(1024)S(1)} %fusion.83) | copy-start | bytes 9460
  59.4 54.0 %copy-start.19 = (s32[788]{0:T(1024)}, s32[788]{0:T(1024)S(1)}, u32[]{:S(2)}) copy-start(s32[788]{0:T(1024)S(1)} %get-tuple-element.29) | copy-start | bytes 9460
  59.4 54.0 %copy-start.21 = (s32[788]{0:T(1024)}, s32[788]{0:T(1024)S(1)}, u32[]{:S(2)}) copy-start(s32[788]{0:T(1024)S(1)} %get-tuple-element.30) | copy-start | bytes 9460
  106.1 48.6 %copy-start.4 = (pred[788,788]{0,1:T(8,128)(4,1)}, pred[788,788]{0,1:T(8,128)(4,1)S(1)}, u32[]{:S(2)}) copy-start(pred[788,788]{0,1:T(8,128)(4,1)S(1)} %broadcast_compare_fusion) | copy-start | bytes 1862836
  106.2 7.1 copy-start.29
  106.3 7.1 copy-start.31
  106.4 7.1 copy-start.33
  106.4 7.1 copy-start.35
  139.1 15.6 %copy-start.15 = (f32[12,788]{1,0:T(8,128)}, f32[12,788]{1,0:T(8,128)S(1)}, u32[]{:S(2)}) copy-start(f32[12,788]{1,0:T(8,128)S(1)} %get-tuple-element.65) | copy-start | bytes 113476
  154.7 0.6 copy-start.17
  176.7 253.8 %copy-start = (f32[788,768]{1,0:T(8,128)}, f32[788,768]{1,0:T(8,128)S(1)}, u32[]{:S(2)}) copy-start(f32[788,768]{1,0:T(8,128)S(1)} %get-tuple-element.68) | copy-start | bytes 7262212
  177.1 10.8 %copy-start.27 = (f32[788]{0:T(1024)}, f32[788]{0:T(1024)S(1)}, u32[]{:S(2)}) copy-start(f32[788]{0:T(1024)S(1)} %multiply_reduce_fusion.3) | copy-start | bytes 9460
  207.2 5.2 copy-start.50
  207.2 6.5 copy-start.47
  207.2 14.4 %copy-start.44 = (bf16[1,768]{1,0:T(2,128)(2,1)S(1)}, bf16[1,768]{1,0:T(2,128)(2,1)}, u32[]{:S(2)}) copy-start(bf16[1,768]{1,0:T(2,128)(2,1)} %param.32) | copy-start | bytes 4612
  207.2 74.1 %all-to-all-start = ((bf16[8,246,768]{2,1,0:T(8,128)(2,1)}), bf16[8,246,768]{2,1,0:T(8,128)(2,1)}, u32[]{:S(2)}, u32[]{:S(2)}) async-start(bf16[8,246,768]{2,1,0:T(8,128)(2,1)} %reshape.308), calls=%async_computation | async-start | bytes 6094848 | tf_op jit(solution)/shard_map/all_to_all | solution.py:191
  211.8 96.7 %all-gather.13.cloned.1.call-start = ((), (), s32[]{:S(2)}) async-start(), calls=%async_computation.13 | async-start | bytes 5898240 | tf_op jit(solution)/shard_map/all_gather | solution.py:147
  327.0 4.7 copy-start.46
  327.0 105.5 %all-to-all-start.1 = ((bf16[8,246,768]{2,1,0:T(8,128)(2,1)}), bf16[8,246,768]{2,1,0:T(8,128)(2,1)}, u32[]{:S(2)}, u32[]{:S(2)}) async-start(bf16[8,246,768]{2,1,0:T(8,128)(2,1)} %reshape.310), calls=%async_computation.1 | async-start | bytes 6094848 | tf_op jit(solution)/shard_map/all_to_all | solution.py:208
  331.6 501.2 %reduce-scatter.23.cloned.1.call-start = ((), (), s32[]{:S(2)}) async-start(), calls=%async_computation.19 | async-start | bytes 245760
  431.0 1.0 copy-start.9
  446.1 3.2 copy-start.34
  446.1 3.2 copy-start.36
  446.1 3.2 copy-start.30
  446.1 3.2 copy-start.32
  446.1 3.2 copy-start.20
  446.1 3.2 copy-start.22
  446.1 3.3 copy-start.2
  553.3 281.0 %reduce-scatter.21.cloned.1.call-start = ((), (), s32[]{:S(2)}) async-start(), calls=%async_computation.18 | async-start | bytes 983040
  555.7 33.6 %copy-start.14 = (bf16[1968,768]{1,0:T(8,128)(2,1)S(1)}, bf16[1968,768]{1,0:T(8,128)(2,1)}, u32[]{:S(2)}) copy-start(bf16[1968,768]{1,0:T(8,128)(2,1)} %reshape.313) | copy-start | bytes 9068548
  589.1 303.2 %reduce-scatter.19.cloned.1.call-start = ((), (), s32[]{:S(2)}) async-start(), calls=%async_computation.17 | async-start | bytes 5898240 | tf_op jit(solution)/shard_map/reduce_scatter | solution.py:267
  619.7 3.8 copy-start.16
  619.7 3.8 copy-start.18
  619.7 73.1 %all-to-all-start.3 = ((bf16[8,246,768]{2,1,0:T(8,128)(2,1)}), bf16[8,246,768]{2,1,0:T(8,128)(2,1)S(1)}, u32[]{:S(2)}, u32[]{:S(2)}) async-start(bf16[8,246,768]{2,1,0:T(8,128)(2,1)} %reshape.314), calls=%async_computation.3 | async-start | bytes 6094848 | tf_op jit(solution)/shard_map/all_to_all | solution.py:274
  623.5 271.6 %reduce-scatter.17.cloned.1.call-start = ((), (), s32[]{:S(2)}) async-start(), calls=%async_computation.16 | async-start | bytes 5898240 | tf_op jit(solution)/shard_map/reduce_scatter | solution.py:261
  639.0 261.3 %reduce-scatter.15.cloned.1.call-start = ((), (), s32[]{:S(2)}) async-start(), calls=%async_computation.15 | async-start | bytes 2433024 | tf_op jit(solution)/shard_map/reduce_scatter | solution.py:313
  705.1 3.9 copy-start.28
  705.1 3.9 copy-start.1
  705.1 3.9 copy-start.10
  705.1 3.9 copy-start.11
  709.1 2.7 copy-start.3
  711.8 1.4 copy-start.6
  711.8 2.2 copy-start.49
  720.6 1.8 copy-start.5
  803.2 222.3 %reduce-scatter.13.cloned.1.call-start = ((), (), s32[]{:S(2)}) async-start(), calls=%async_computation.14 | async-start | bytes 7299072 | tf_op jit(solution)/shard_map/reduce_scatter | solution.py:311
  819.6 4.8 copy-start.8
  819.6 4.8 copy-start.24
  819.6 4.8 copy-start.38
  819.6 4.8 copy-start.40
  819.6 4.8 copy-start.43
  822.3 2.1 copy-start.13
  836.1 7.1 copy-start.26
  843.3 1.4 copy-start.12
Sparse Core Ops, SparseCore 0:
  11.1 63.2 all-gather.6
  77.4 52.9 all-gather.8
  132.2 56.0 all-gather.10
  214.2 57.7 all-gather.12
  553.4 22.1 reduce-scatter.22
  589.2 24.2 reduce-scatter.20
  616.5 57.0 reduce-scatter.18
  676.6 57.0 reduce-scatter.16
  803.3 96.9 reduce-scatter.14
  907.3 118.1 reduce-scatter.12
where the time goes:
time: 1040 us; the launch traced here: 1030 us
  blocking collectives  309 us (30%)
  matrix products  257 us (25%)
  waiting for transfers between devices  235 us (23%)
  other arithmetic  122 us (12%)
  local copies, waits for them, and re-layouts  79 us (8%)
  between operations  16.7 us (2%)
  starting transfers between devices  14.2 us (1%)
    reduce_scatter x1, waiting for transfers between devices, local(): lax.psum_scatter(qkv_weight_grad, ('dp', 'expert'), scatter_dimension=0,...  125 us
    all_gather x1, blocking collectives, local(): lax.all_gather(router_weight, ('dp', 'expert'), axis=0, tiled=True)  98.6 us
    unnamed x3, blocking collectives  88 us
    all_to_all x1, blocking collectives, local(): lax.all_to_all(slot_grad, 'expert', split_axis=0, concat_axis=0, tiled=True)  73 us
    dot_general x5, matrix products, contract_cols(): lax.dot_general(left, right, (((1,), (1,)), ((), ())), preferred_element_...  60.7 us
    all_to_all x1, waiting for transfers between devices, local(): lax.all_to_all(buffer_grad.reshape(incoming.shape), 'expert', split_axis=...  53.6 us
    all_to_all x1, waiting for transfers between devices, local(): lax.all_to_all(outgoing.reshape(expert_count, slot_cap, model_width), 'ex...  50.8 us
    dot_general x5, matrix products, contract_rows(): lax.dot_general(left, right, (((0,), (0,)), ((), ())), preferred_element_...  40.9 us
  transfers between devices with their start and end apart: 13, of which 4 were waited for; matrix products, arithmetic and copies ran while one was open for 37% of the time, Pallas kernels for 0%

commit v1 on v0

v1 whole, which is shorter than its diff:
```python
import functools

import jax
import jax.numpy as jnp
from jax import lax
from jax.experimental import pallas as pl
from jax.experimental.pallas import tpu as pltpu
from jax.sharding import PartitionSpec as P

HEADS = 12
SEQ = 197
EPS_NORM = 1e-06
NEG_FILL = -1e30
BF = jnp.bfloat16
F32 = jnp.float32
LANES = 128
GELU_A = 0.7978845608028654
GELU_B = 0.044715
BOTH = ("dp", "expert")


def up16(n):
    return -(-n // 16) * 16


def dot(left, right):
    return jnp.dot(left, right, preferred_element_type=F32)


def dot_t(left, right):
    return lax.dot_general(left, right, (((1,), (1,)), ((), ())), preferred_element_type=F32)


def t_dot(left, right):
    return lax.dot_general(left, right, (((0,), (0,)), ((), ())), preferred_element_type=F32)


def iota(shape, dim):
    return lax.broadcasted_iota(jnp.int32, shape, dim)


def params(mib=60):
    return pltpu.CompilerParams(vmem_limit_bytes=mib << 20)


def whole(shape):
    zeros = (0,) * len(shape)
    return pl.BlockSpec(shape, lambda *_: zeros, pipeline_mode=pl.Buffered(1))


SMALL = pl.CostEstimate(flops=1 << 20, bytes_accessed=1 << 16, transcendentals=0)
SMEM = pl.BlockSpec(memory_space=pltpu.SMEM)
ANY = pl.BlockSpec(memory_space=pl.ANY)


def norm_stats(values):
    centered = values - jnp.mean(values, axis=-1, keepdims=True)
    inverse = lax.rsqrt(jnp.mean(centered * centered, axis=-1, keepdims=True) + EPS_NORM)
    return centered * inverse, inverse


def norm_back(unit, inverse, gain, grad):
    scaled = grad * gain
    mean_one = jnp.mean(scaled, axis=-1, keepdims=True)
    mean_two = jnp.mean(scaled * unit, axis=-1, keepdims=True)
    return inverse * (scaled - mean_one - unit * mean_two)


def col_sum(values):
    return jnp.sum(values, axis=0, keepdims=True)


def pack_kernel(experts, core, qkv, out, router, vectors, mine, other):
    rows = qkv.shape[0]
    eye = (iota((rows, rows), 0) == iota((rows, rows), 1)).astype(BF)
    turned = dot_t(eye, vectors[...]).astype(BF)
    fill = jnp.zeros((rows, 2 * LANES - experts - turned.shape[1]), BF)
    value = jnp.concatenate([qkv[...], out[...], router[...], turned, fill], axis=1)
    half = value.shape[1] // 2

    @pl.when(core[0] == 0)
    def _():
        mine[...] = value[:, :half]
        other[...] = value[:, half:]

    @pl.when(core[0] != 0)
    def _():
        mine[...] = value[:, half:]
        other[...] = value[:, :half]


def pack_dense(core, qkv, out, router, vectors):
    rows = qkv.shape[0]
    half = (qkv.shape[1] + out.shape[1] + 2 * LANES) // 2
    vmem = pl.BlockSpec(memory_space=pltpu.VMEM)
    return pl.pallas_call(
        functools.partial(pack_kernel, router.shape[1]),
        in_specs=[SMEM] + [vmem] * 4,
        out_specs=[vmem] * 2,
        out_shape=[jax.ShapeDtypeStruct((rows, half), BF)] * 2,
        compiler_params=params(),
        cost_estimate=SMALL,
        name="pack_dense",
    )(core, qkv, out, router, vectors)


def forward_kernel(experts, subs, off, count, tok, *refs):
    n_pieces = len(refs) - 9
    pieces = refs[:n_pieces]
    w, small, qkv_o, n1_o, att_o, aa_o, n2_o, prob_o, sems = refs[n_pieces:]
    img = pl.program_id(0)
    width = tok.shape[-1]

    @pl.when(img == 0)
    def _():
        copies = []
        for i, piece in enumerate(pieces):
            rows, cols = piece.shape[0] // subs, piece.shape[1]
            col = pl.multiple_of(off[n_pieces * subs + i], LANES)
            for j in range(subs):
                row = pl.multiple_of(off[i * subs + j], 16)
                copies.append(
                    pltpu.make_async_copy(
                        piece.at[pl.ds(j * rows, rows), :],
                        w.at[pl.ds(row, rows), pl.ds(col, cols)],
                        sems.at[i * subs + j],
                    )
                )
        for c in copies:
            c.start()
        for c in copies:
            c.wait()
        small[...] = jnp.transpose(w[:, 4 * width : 4 * width + LANES].astype(F32))

    def vec(k):
        return small[experts + k : experts + k + 1, :]

    x = tok[0].astype(F32)
    rows = x.shape[0]
    unit, _ = norm_stats(x)
    n1 = (unit * vec(0) + vec(1)).astype(BF)
    n1_o[0] = n1
    biases = (vec(5), None, vec(6))
    for part in range(3):
        cols = slice(part * width, (part + 1) * width)
        block = dot(n1, w[:, cols])
        if biases[part] is not None:
            block = block + biases[part]
        qkv_o[0, :, cols] = block.astype(BF)
    low = iota((rows, LANES), 1) < LANES // 2
    seen = iota((rows, rows), 1) < SEQ
    scale = (width // HEADS) ** -0.5
    for pair in range(HEADS // 2):
        c = pair * LANES
        q2 = qkv_o[0, :, c : c + LANES]
        k2 = qkv_o[0, :, width + c : width + c + LANES]
        v2 = qkv_o[0, :, 2 * width + c : 2 * width + c + LANES]
        got = []
        for side, mask in enumerate((low, ~low)):
            scores = dot_t(jnp.where(mask, q2, jnp.zeros_like(q2)), k2) * scale
            scores = jnp.where(seen, scores, NEG_FILL)
            exps = jnp.exp(scores - jnp.max(scores, axis=-1, keepdims=True))
            prob = exps * (1.0 / jnp.sum(exps, axis=-1, keepdims=True))
            prob_o[0, 2 * pair + side] = prob
            got.append(dot(prob.astype(BF), v2))
        att_o[0, :, c : c + LANES] = jnp.where(low, got[0], got[1]).astype(BF)
    alive = (img < count[0]).astype(F32)
    after = x + alive * (dot(att_o[0], w[:, 3 * width : 4 * width]) + vec(2))
    aa_o[0] = after
    unit, _ = norm_stats(after)
    n2_o[0] = (unit * vec(3) + vec(4)).astype(BF)


def forward(off, subs, pieces, count, tok, experts, width_all):
    images, rows, width = tok.shape
    block = lambda cols: pl.BlockSpec((1, rows, cols), lambda i: (i, 0, 0))
    shape = lambda cols, t: jax.ShapeDtypeStruct((images, rows, cols), t)
    return pl.pallas_call(
        functools.partial(forward_kernel, experts, subs),
        grid=(images,),
        in_specs=[SMEM, SMEM, block(width)] + [ANY] * len(pieces),
        out_specs=[
            whole((width, width_all)),
            whole((LANES, width)),
            block(3 * width),
            block(width),
            block(width),
            block(width),
            block(width),
            pl.BlockSpec((1, HEADS, rows, rows), lambda i: (i, 0, 0, 0)),
        ],
        out_shape=[
            jax.ShapeDtypeStruct((width, width_all), BF),
            jax.ShapeDtypeStruct((LANES, width), F32),
            shape(3 * width, BF),
            shape(width, BF),
            shape(width, BF),
            shape(width, F32),
            shape(width, BF),
            jax.ShapeDtypeStruct((images, HEADS, rows, rows), F32),
        ],
        scratch_shapes=[pltpu.SemaphoreType.DMA((len(pieces) * subs,))],
        compiler_params=params(),
        cost_estimate=SMALL,
        name="tokens_forward",
    )(off, count, tok, *pieces)


def dispatch_kernel(experts, half, gated, slots, x, *refs):
    out = refs[-1]
    value = x[...]
    halves, block_rows = out.shape[1:3]
    first, second = slots[0:1, :], slots[1:2, :]
    if gated:
        router = refs[0][...].astype(BF)
        logits = dot_t(router, value)
        logits = jnp.where(iota(logits.shape, 0) < experts, logits, NEG_FILL)
        exps = jnp.exp(logits - jnp.max(logits, axis=0, keepdims=True))
        probs = exps / jnp.sum(exps, axis=0, keepdims=True)
    total = experts * block_rows
    for h in range(halves):
        place = iota((total, value.shape[0]), 0) + (half + h) * total
        hot = ((place == first) | (place == second)).astype(BF)
        out[:, h] = dot(hot, value).astype(BF).reshape(experts, block_rows, value.shape[1])
        if gated:
            row = iota((16, value.shape[0]), 0)
            for e in range(experts):
                gate = probs[e : e + 1, :]
                high = gate.astype(BF).astype(F32)
                pair = jnp.where(row == 14, high, jnp.where(row == 15, gate - high, 0.0))
                placed = dot_t(pair.astype(BF), hot[e * block_rows : (e + 1) * block_rows])
                tail = out[e, h, block_rows - 16 :, :block_rows].astype(F32)
                out[e, h, block_rows - 16 :, :block_rows] = jnp.where(
                    iota(tail.shape, 0) < 14, tail, placed
                ).astype(BF)


def dispatch(slots, x, small, experts, block_rows, half, halves, tag):
    rows, width = x.shape
    gated = small is not None
    more = [small] if gated else []
    vmem = pl.BlockSpec(memory_space=pltpu.VMEM)
    return pl.pallas_call(
        functools.partial(dispatch_kernel, experts, half, gated),
        in_specs=[vmem] * (2 + len(more)),
        out_specs=vmem,
        out_shape=jax.ShapeDtypeStruct((experts, halves, block_rows, width), BF),
        compiler_params=params(),
        cost_estimate=SMALL,
        name="dispatch_" + tag,
    )(slots, x, *more)


def expert_kernel(parts, n_before, *refs):
    x_ref, c_ref, b_in, b_out = refs[:4]
    pieces_in, pieces_out = refs[4 : 4 + parts], refs[4 + parts : 4 + 2 * parts]
    rest = refs[4 + 2 * parts + n_before :]
    act_o, pre_o, x_o, sg_o, r_o, d_o, db_in, db_out, win, wout, sems = rest
    step = pl.program_id(0)
    n, _, size, width = x_ref.shape
    piece = pieces_in[0].shape[1]

    def copies(q):
        cols = pl.ds(q * piece, piece)
        return (
            pltpu.make_async_copy(pieces_in[q], win.at[:, cols], sems.at[q]),
            pltpu.make_async_copy(pieces_out[q], wout.at[cols, :], sems.at[parts + q]),
        )

    @pl.when(step == 0)
    def _():
        for q in range(parts):
            for c in copies(q):
                c.start()
        db_in[...] = jnp.zeros_like(db_in)
        db_out[...] = jnp.zeros_like(db_out)

    eye = (iota((size, size), 0) == iota((size, size), 1)).astype(BF)
    for s in range(n):
        rows = slice(s * size, (s + 1) * size)
        x_o[rows, :] = x_ref[s, 0]
        turned = dot_t(eye, x_ref[s, 0, size - 16 :, :size])
        gate = jnp.sum(jnp.where(iota(turned.shape, 1) >= 14, turned, 0.0), axis=1, keepdims=True)
        sg_o[rows, :] = (gate * c_ref[s, 0].astype(F32)).astype(BF)
    x = x_o[...]
    slot_grad = sg_o[...]
    db_out[0:1, :] += col_sum(slot_grad.astype(F32))

    @pl.when(step == 0)
    def _():
        for q in range(parts):
            for c in copies(q):
                c.wait()

    for q in range(parts):
        cols = slice(q * piece, (q + 1) * piece)
        pre = dot(x, win[:, cols]) + b_in[q, 0:1, :]
        square = pre * pre
        turn = jnp.tanh(pre * (GELU_A + GELU_A * GELU_B * square))
        half_turn = 0.5 * turn + 0.5
        act_o[:, cols] = (pre * half_turn).astype(BF)
        slope = half_turn + (0.5 * pre) * (1.0 - turn * turn) * (GELU_A + 3 * GELU_A * GELU_B * square)
        pre_grad = dot_t(slot_grad, wout[cols, :]) * slope
        pre_o[:, cols] = pre_grad.astype(BF)
        db_in[q, 0:1, :] += col_sum(pre_grad)
    out = (dot(act_o[...], wout[...]) + b_out[0:1, :]).astype(BF)
    back = dot_t(pre_o[...], win[...])
    ones = jnp.ones((16, width), BF)
    for s in range(n):
        rows = slice(s * size, (s + 1) * size)
        r_o[s, 0] = out[rows]
        d_o[s] = back[rows].astype(BF)
        prod = c_ref[s, 0].astype(F32) * out[rows].astype(F32)
        high = prod.astype(BF)
        low = (prod - high.astype(F32)).astype(BF)
        gate_grad = dot_t(ones, high) + dot_t(ones, low)
        grad_high = gate_grad.astype(BF).astype(F32)
        row = iota(gate_grad.shape, 0)
        tail = back[(s + 1) * size - 16 : (s + 1) * size, :size]
        both = jnp.where(row == 14, grad_high, gate_grad - grad_high)
        d_o[s, size - 16 :, :size] = jnp.where(row < 14, tail, both).astype(BF)


def expert_call(x, c, w_in, w_out, b_in, b_out, half, halves, before):
    experts, _, size, width = x.shape
    parts, piece = len(w_in), w_in[0].shape[1]
    n = max(1, 256 // size)
    steps = experts // n
    rows, hidden = n * size, parts * piece
    before = list(before)
    tall = lambda cols: pl.BlockSpec((rows, cols), lambda i: (half * steps + i, 0))
    of_half = pl.BlockSpec((n, 1, size, width), lambda i: (i, half, 0, 0))
    total = halves * experts * size
    return pl.pallas_call(
        functools.partial(expert_kernel, parts, len(before)),
        grid=(steps,),
        in_specs=[
            pl.BlockSpec((n, 1, size, width), lambda i: (i, 0, 0, 0)),
            of_half,
            whole((parts, 8, piece)),
            whole((8, width)),
        ]
        + [ANY] * (2 * parts + len(before)),
        out_specs=[
            tall(hidden),
            tall(hidden),
            tall(width),
            tall(width),
            of_half,
            pl.BlockSpec((n, size, width), lambda i: (i, 0, 0)),
            whole((parts, 8, piece)),
            whole((8, width)),
        ],
        out_shape=[
            jax.ShapeDtypeStruct((total, hidden), BF),
            jax.ShapeDtypeStruct((total, hidden), BF),
            jax.ShapeDtypeStruct((total, width), BF),
            jax.ShapeDtypeStruct((total, width), BF),
            jax.ShapeDtypeStruct((experts, halves, size, width), BF),
            jax.ShapeDtypeStruct((experts, size, width), BF),
            jax.ShapeDtypeStruct((parts, 8, piece), F32),
            jax.ShapeDtypeStruct((8, width), F32),
        ],
        scratch_shapes=[
            pltpu.VMEM((width, hidden), BF),
            pltpu.VMEM((hidden, width), BF),
            pltpu.SemaphoreType.DMA((2 * parts,)),
        ],
        input_output_aliases={4 + 2 * parts + i: i for i in range(len(before))},
        compiler_params=params(),
        cost_estimate=SMALL,
        name="expert_" + "ab"[half],
    )(x, c, b_in, b_out, *w_in, *w_out, *before)


def backward_kernel(experts, n, split, off, count, slots, cot, n1, qkv, att, aa, n2, probs_in, w, small, *refs):
    backs = refs[:n]
    ag_o, gp_o, dq_o = refs[n : n + 3]
    grads = refs[n + 3 : n + 3 + split]
    dw, ds, marks = refs[n + 3 + split :]
    img = pl.program_id(0)
    width = n1.shape[-1]
    size = backs[0].shape[1]
    total = experts * size

    @pl.when(img == 0)
    def _():
        dw[...] = jnp.zeros_like(dw)
        ds[...] = jnp.zeros_like(ds)
        line = iota((LANES, size), 0)
        for h in range(n):
            for e in range(experts):
                ends = backs[h][e, size - 16 :, :size].astype(F32)
                for k in range(2):
                    marks[2 * h + k, :, e * size : (e + 1) * size] = jnp.where(
                        line == e, ends[14 + k : 15 + k, :], 0.0
                    ).astype(BF)

    def vec(k):
        return small[experts + k : experts + k + 1, :]

    def add_vec(k, value):
        ds[experts + k : experts + k + 1, :] += value

    alive = (img < count[0]).astype(F32)
    up = cot[0].astype(F32)
    rows = up.shape[0]
    normed = n2[0]
    lane = iota((rows, LANES), 1)
    router = jnp.where(iota(small.shape, 0) < experts, small[...], 0.0).astype(BF)
    logits = jnp.where(lane < experts, dot_t(normed, router), NEG_FILL)
    exps = jnp.exp(logits - jnp.max(logits, axis=-1, keepdims=True))
    probs = exps / jnp.sum(exps, axis=-1, keepdims=True)
    gp_o[0] = probs
    first, second = slots[0, :, 0:1], slots[0, :, 1:2]
    normed_grad = jnp.zeros((rows, width), F32)
    placed = jnp.zeros((rows, LANES), F32)
    for h in range(n):
        place = iota((rows, total), 1) + h * total
        hot = ((place == first) | (place == second)).astype(BF)
        normed_grad = normed_grad + dot(hot, backs[h][...].reshape(total, width))
        placed = placed + dot_t(hot, marks[2 * h]) + dot_t(hot, marks[2 * h + 1])
    logit_grad = (
        probs * (placed - jnp.sum(probs * placed, axis=-1, keepdims=True))
    ).astype(BF)
    normed_grad = normed_grad + dot(logit_grad, router)
    ds[...] += jnp.where(iota(ds.shape, 0) < experts, t_dot(logit_grad, normed), 0.0)
    unit, inverse = norm_stats(aa[0])
    add_vec(3, col_sum(normed_grad * unit))
    add_vec(4, col_sum(normed_grad))
    after_grad = up + norm_back(unit, inverse, vec(3), normed_grad)
    attn_grad = (alive * after_grad).astype(BF)
    add_vec(2, col_sum(attn_grad.astype(F32)))
    dw[:, 3 * width : 4 * width] += t_dot(att[0], attn_grad)
    att_grad = dot_t(attn_grad, w[:, 3 * width : 4 * width]).astype(BF)
    low = lane < LANES // 2
    scale = (width // HEADS) ** -0.5
    for pair in range(HEADS // 2):
        c = pair * LANES
        q2 = qkv[0, :, c : c + LANES]
        k2 = qkv[0, :, width + c : width + c + LANES]
        v2 = qkv[0, :, 2 * width + c : 2 * width + c + LANES]
        o2 = att_grad[:, c : c + LANES]
        got = []
        for side, mask in enumerate((low, ~low)):
            prob = probs_in[0, 2 * pair + side]
            prob_grad = dot_t(jnp.where(mask, o2, jnp.zeros_like(o2)), v2)
            inner = jnp.sum(prob * prob_grad, axis=-1, keepdims=True)
            score_grad = (prob * (prob_grad - inner)).astype(BF)
            got.append(
                (
                    dot(score_grad, k2) * scale,
                    t_dot(score_grad, q2) * scale,
                    t_dot(prob.astype(BF), o2),
                )
            )
        for k in range(3):
            dq_o[0, :, k * width + c : k * width + c + LANES] = jnp.where(
                low, got[0][k], got[1][k]
            ).astype(BF)
    grad = dq_o[0]
    dw[:, : 3 * width] += t_dot(n1[0], grad)
    for k in range(3):
        ds[experts + 5 + k : experts + 6 + k, :] += col_sum(grad[:, k * width : (k + 1) * width].astype(F32))
    ag_o[0] = after_grad

    @pl.when(img == pl.num_programs(0) - 1)
    def _():
        dw[:, 4 * width : 4 * width + LANES] = jnp.transpose(ds[...])
        with_weight = jnp.zeros((width, LANES), F32)
        with_sums = jnp.zeros((width, LANES), F32)
        for k in range(3 * width // LANES):
            cols = slice(k * LANES, (k + 1) * LANES)
            part, at = divmod(k * LANES, width)
            value = w[:, cols].astype(F32)
            sums = ds[experts + 5 + part : experts + 6 + part, at : at + LANES]
            with_weight = with_weight + value * dw[:, cols]
            with_sums = with_sums + value * sums
        sums = jnp.sum(with_sums, axis=1, keepdims=True)
        at = 4 * width
        sides = w[:, at : at + LANES].astype(F32)
        gain, shift = sides[:, experts : experts + 1], sides[:, experts + 1 : experts + 2]
        gains = (jnp.sum(with_weight, axis=1, keepdims=True) - shift * sums) / gain
        spot = iota((width, LANES), 1)
        cols = slice(at, at + LANES)
        dw[:, cols] = jnp.where(
            spot == experts, gains, jnp.where(spot == experts + 1, sums, dw[:, cols])
        )
        if split == 1:
            grads[0][...] = dw[...].astype(BF)
        else:
            cols = grads[0].shape[1]
            step = width // 16
            for h in range(2):
                col = pl.multiple_of(off[16 + h], LANES)
                for r in range(16):
                    row = pl.multiple_of(off[r], 16)
                    grads[h][r * step : (r + 1) * step, :] = dw[
                        pl.ds(row, step), pl.ds(col, cols)
                    ].astype(BF)


def backward(off, count, slots, cot, n1, qkv, att, aa, n2, prob, w, small, backs, experts, split):
    images, rows, width = cot.shape
    width_all = w.shape[1]
    n = len(backs)
    block = lambda cols: pl.BlockSpec((1, rows, cols), lambda i: (i, 0, 0))
    got = pl.pallas_call(
        functools.partial(backward_kernel, experts, n, split),
        grid=(images,),
        in_specs=[SMEM, SMEM, block(2), block(width), block(width), block(3 * width), block(width), block(width), block(width)]
        + [pl.BlockSpec((1, HEADS, rows, rows), lambda i: (i, 0, 0, 0))]
        + [whole(w.shape), whole(small.shape)]
        + [whole(backs[0].shape)] * n,
        out_specs=[block(width), block(LANES), block(3 * width)] + [whole((width, width_all // split))] * split,
        out_shape=[
            jax.ShapeDtypeStruct((images, rows, width), F32),
            jax.ShapeDtypeStruct((images, rows, LANES), F32),
            jax.ShapeDtypeStruct((images, rows, 3 * width), BF),
        ]
        + [jax.ShapeDtypeStruct((width, width_all // split), BF)] * split,
        scratch_shapes=[
            pltpu.VMEM((width, width_all), F32),
            pltpu.VMEM((LANES, width), F32),
            pltpu.VMEM((2 * n, LANES, backs[0].shape[0] * backs[0].shape[1]), BF),
        ],
        compiler_params=params(),
        cost_estimate=SMALL,
        name="tokens_backward",
    )(off, count, slots, cot, n1, qkv, att, aa, n2, prob, w, small, *backs)
    return got[0], got[1], got[2], got[3:]


def finish_kernel(experts, after_grad, grad, tok, w, small, out):
    width = tok.shape[-1]
    normed_grad = dot_t(grad[0], w[...])
    unit, inverse = norm_stats(tok[0].astype(F32))
    out[0] = after_grad[0] + norm_back(unit, inverse, small[experts : experts + 1, :], normed_grad)


def finish(after_grad, grad, tok, w, small, experts):
    images, rows, width = tok.shape
    block = lambda cols: pl.BlockSpec((1, rows, cols), lambda i: (i, 0, 0))
    return pl.pallas_call(
        functools.partial(finish_kernel, experts),
        grid=(images,),
        in_specs=[block(width), block(3 * width), block(width), whole((width, 3 * width)), whole(small.shape)],
        out_specs=block(width),
        out_shape=jax.ShapeDtypeStruct((images, rows, width), F32),
        compiler_params=params(),
        cost_estimate=SMALL,
        name="tokens_finish",
    )(after_grad, grad, tok, w, small)


def output_kernel(count, slots, aa, probs, outs, out):
    rows = aa.shape[1]
    experts, n, size, width = outs.shape
    total = experts * size
    alive = (pl.program_id(0) < count[0]).astype(F32)
    first, second = slots[0, :, 0:1], slots[0, :, 1:2]
    gates = jnp.concatenate(
        [jnp.broadcast_to(probs[0, :, e : e + 1], (rows, size)) for e in range(experts)], axis=1
    )
    moe = jnp.zeros(aa.shape[1:], F32)
    for h in range(n):
        place = iota((rows, total), 1) + h * total
        gate = jnp.where((place == first) | (place == second), gates, 0.0)
        high = gate.astype(BF)
        low = (gate - high.astype(F32)).astype(BF)
        value = outs[:, h].reshape(total, width)
        moe = moe + dot(high, value) + dot(low, value)
    out[0] = (aa[0] + alive * moe).astype(BF)


def block_output(count, slots, aa, probs, outs):
    images, rows, width = aa.shape
    block = lambda cols: pl.BlockSpec((1, rows, cols), lambda i: (i, 0, 0))
    return pl.pallas_call(
        output_kernel,
        grid=(images,),
        in_specs=[SMEM, block(2), block(width), block(LANES), whole(outs.shape)],
        out_specs=block(width),
        out_shape=jax.ShapeDtypeStruct((images, rows, width), BF),
        compiler_params=params(),
        cost_estimate=SMALL,
        name="block_output",
    )(count, slots, aa, probs, outs)


def slot_tables(routes, alive, capacity, half_cap, block_rows):
    expert_ids = jnp.arange(capacity.shape[0], dtype=jnp.int32)
    count = routes.shape[0]
    hit_one = ((routes[:, 0:1] == expert_ids) & alive[:, None]).astype(F32)
    hit_two = ((routes[:, 1:2] == expert_ids) & alive[:, None]).astype(F32)
    earlier = (iota((count, count), 1) < iota((count, count), 0)).astype(BF)
    ahead = dot(earlier, jnp.concatenate([hit_one, hit_two], axis=1).astype(BF))
    ahead_one = ahead[:, : capacity.shape[0]]
    ahead_two = ahead[:, capacity.shape[0] :] + jnp.sum(hit_one, axis=0, keepdims=True)
    limits = capacity.astype(F32)[None, :]
    slots = []
    for hit, before, choice in ((hit_one, ahead_one, 0), (hit_two, ahead_two, 1)):
        place = jnp.sum(hit * before, axis=1)
        keep = place < jnp.sum(hit * limits, axis=1)
        place = place.astype(jnp.int32)
        half = (place >= half_cap).astype(jnp.int32)
        spot = (half * capacity.shape[0] + routes[:, choice]) * block_rows + place - half * half_cap
        slots.append(jnp.where(keep, spot, -1))
    return jnp.stack(slots, axis=1), jnp.stack(slots, axis=0)


def local(sizes, *args):
    (tokens, image_count, routes, capacity, ln1_gain, ln1_bias, qkv_weight, qv_bias, out_weight, out_bias,
     ln2_gain, ln2_bias, router_weight, expert_in, expert_in_bias, expert_out, expert_out_bias, cotangent) = args
    dp, experts = sizes
    grouped = sizes == (4, 8)
    devices = dp * experts
    me_d = lax.axis_index("dp")
    me_e = lax.axis_index("expert")
    core = me_e % 2
    token_count, width = tokens.shape
    images = token_count // SEQ
    rows = up16(SEQ)
    cap = max(2, 5 * token_count // (2 * experts))
    halves = 2 if grouped else 1
    half_cap = -(-cap // halves)
    block_rows = up16(half_cap + 2)

    def hop(value, mask):
        return lax.ppermute(value, BOTH, [(i, i ^ mask) for i in range(devices)])

    def by_image(value):
        value = value.reshape(images, SEQ, value.shape[-1])
        fill = -1 if value.dtype == jnp.int32 else 0
        return jnp.pad(value, ((0, 0), (0, rows - SEQ), (0, 0)), constant_values=fill)

    def from_image(value):
        return value[:, :SEQ].reshape(token_count, value.shape[-1])

    def after(values, *done):
        return lax.optimization_barrier((values, done))[0]

    tok = by_image(tokens)

    vectors = [ln1_gain, ln1_bias, out_bias, ln2_gain, ln2_bias, qv_bias.reshape(-1)]
    vectors = jnp.concatenate(vectors).reshape(7, -1)
    width_all = 4 * width + 2 * LANES
    wide = expert_in.shape[2]
    spot = me_d * expert_out_bias.shape[1]
    if grouped:
        half = width_all // 2
        mine, other = pack_dense(
            core.reshape(1).astype(jnp.int32), qkv_weight, out_weight, router_weight, vectors
        )
        got = hop(other, 1)
        chip = jnp.where(
            core == 0, jnp.concatenate([mine, got], axis=0), jnp.concatenate([got, mine], axis=0)
        )
        in_x, out_y = hop(expert_in[0], 8), hop(expert_out[0], 16)
        line = jnp.concatenate([chip] + [hop(chip, 2 * dz) for dz in (1, 2, 3)], axis=0)
        held, in_x, out_y, tok = after((line, in_x, out_y, tok))
        own = [line] + [hop(held, 8 * dxy) for dxy in (3, 1, 2)]
        own = [own[0], own[2], own[3], own[1]]
        pieces = own + [hop(piece, 1) for piece in own]
        step = width // 16
        at_rows = jnp.stack([((me_d ^ a) * 4 + ((me_e // 2) ^ b)) * step for a in range(4) for b in range(4)])
        at_cols = jnp.stack([core * half, (1 - core) * half])
        off_back = jnp.concatenate([at_rows, at_cols]).astype(jnp.int32)
        off = jnp.concatenate([at_rows, at_rows, jnp.repeat(at_cols, 4)]).astype(jnp.int32)
        subs = 4
        bias_out = lax.dynamic_update_slice(jnp.zeros((1, width), BF), expert_out_bias, (0, spot))
        bias = jnp.concatenate([expert_in_bias, bias_out, jnp.zeros((6, wide), BF)], axis=0)
        own_in, own_out, relay_in, relay_out, bias = after(
            (expert_in[0], expert_out[0], in_x, out_y, bias), *own
        )
        near = [hop(own_in, 16), hop(own_out, 8)]
        far = [hop(relay_in, 16), hop(relay_out, 8)]
        w_in = [expert_in[0], in_x, near[0], far[0]]
        w_out = [expert_out[0], near[1], out_y, far[1]]
        bias_got = [hop(bias, 8 * q) for q in (1, 2, 3)]
        b_in = jnp.stack([bias] + bias_got).astype(F32)
        far += bias_got
        b_out = jnp.broadcast_to(jnp.sum(b_in[:, 1], axis=0), (8, width))
        after_line = held
    else:
        fill = width_all - 4 * width - experts - 7
        pack = jnp.concatenate(
            [qkv_weight, out_weight, router_weight, vectors.T, jnp.zeros((vectors.shape[1], fill), BF)], axis=1
        )
        pieces = [lax.all_gather(pack, BOTH, axis=0, tiled=True)]
        off = jnp.zeros((2,), jnp.int32)
        off_back = off
        subs = 1
        after_line, near, far = pieces[0], [], []
        w_in = lax.all_gather(expert_in[0], "dp", axis=0, tiled=False)
        w_out = lax.all_gather(expert_out[0], "dp", axis=0, tiled=False)
        w_in, w_out = [w_in[q] for q in range(dp)], [w_out[q] for q in range(dp)]
        b_in = lax.all_gather(jnp.broadcast_to(expert_in_bias, (8, wide)), "dp", axis=0, tiled=False).astype(F32)
        b_out = jnp.broadcast_to(
            lax.all_gather(expert_out_bias, "dp", axis=1, tiled=True).astype(F32), (8, width)
        )

    alive = (jnp.arange(images * rows, dtype=jnp.int32) // rows) < image_count[0]
    slots_col, slots_row = slot_tables(
        by_image(routes).reshape(-1, 2), alive, capacity, half_cap, block_rows
    )
    slots_col = slots_col.reshape(images, rows, 2)

    def exchange(blocks):
        return lax.all_to_all(blocks, "expert", 0, 0, tiled=True)

    cot = by_image(cotangent)
    cot_blocks = dispatch(slots_row, cot.reshape(-1, width), None, experts, block_rows, 0, halves, "plain")
    cot_sent = exchange(after(cot_blocks, after_line))

    w, small, qkv, n1, att, aa, n2, prob = forward(off, subs, pieces, image_count, tok, experts, width_all)
    row_sent = []
    flat = after(n2.reshape(-1, width), *near)
    for h in range(halves):
        sent = dispatch(slots_row, flat, small, experts, block_rows, h, 1, "ab"[h])
        waits = (*row_sent, *far) if h else ()
        sent, cot_sent = after((sent, cot_sent), *waits)
        row_sent.append(exchange(sent))

    back, db_ins, db_outs, tall = [], [], [], ()
    for h in range(halves):
        *tall, d, db_in, db_out = expert_call(
            row_sent[h], cot_sent, w_in, w_out, b_in, b_out, h, halves, tall
        )
        back.append(exchange(after(d, *back)))
        db_ins.append(db_in)
        db_outs.append(db_out)
    *tall, outs_back = tall
    act, pre, rows_in, slot_grad = after(tall, *back[:-1])
    db_in, db_out = sum(db_ins), sum(db_outs)

    def grad_in(q):
        return t_dot(rows_in, pre[:, q * wide : (q + 1) * wide])

    def grad_out(q):
        return t_dot(act[:, q * wide : (q + 1) * wide], slot_grad)

    if grouped:
        far_in, far_out = hop(grad_in(3).astype(BF), 8), hop(grad_out(3).astype(BF), 16)
        near_in, near_out = grad_in(1).astype(BF), grad_out(2).astype(BF)
        own_in, own_out = grad_in(0), grad_out(0)
        last_in = (grad_in(2) + far_in.astype(F32)).astype(BF)
        last_out = (grad_out(1) + far_out.astype(F32)).astype(BF)
        ready = (near_in, near_out, own_in, own_out, last_in, last_out)
        near_in, near_out = hop(near_in, 8), hop(near_out, 16)
        last_in, last_out = hop(last_in, 16), hop(last_out, 8)
        arrived = (near_in, near_out, last_in, last_out)
        g_in = (own_in + near_in.astype(F32) + last_in.astype(F32))[None]
        g_out = (own_out + near_out.astype(F32) + last_out.astype(F32))[None]
        g_bias = [
            jnp.concatenate([db_in[q, 0:1], db_out[0:1], jnp.zeros((6, wide), F32)], axis=0).astype(BF)
            for q in range(4)
        ]
        g_bias = sum([hop(g_bias[q], 8 * q).astype(F32) for q in (1, 2, 3)], g_bias[0].astype(F32))
        g_b_in = g_bias[0:1]
        g_b_out = lax.dynamic_slice(g_bias[1:2], (0, spot), expert_out_bias.shape)
    else:
        ready = arrived = ()
        every = range(dp)
        scatter = lambda v: lax.psum_scatter(v, "dp", scatter_dimension=0, tiled=True).astype(F32)
        g_in = scatter(jnp.stack([grad_in(q).astype(BF) for q in every]))
        g_out = scatter(jnp.stack([grad_out(q).astype(BF) for q in every]))
        g_b_in = lax.psum_scatter(
            db_in[:, 0].reshape(1, -1).astype(BF), "dp", scatter_dimension=1, tiled=True
        ).astype(F32)
        g_b_out = lax.psum_scatter(db_out[0:1].astype(BF), "dp", scatter_dimension=1, tiled=True).astype(F32)

    r_sent = exchange(after(outs_back, *back))
    back = after(back, *ready)
    after_grad, probs, grad, grads = backward(
        off_back, image_count, slots_col, cot, n1, qkv, att, aa, n2, prob, w, small, back, experts,
        2 if grouped else 1,
    )
    grads = after(grads, *arrived)
    block_out = from_image(block_output(image_count, slots_col, aa, probs, r_sent))
    tokens_grad = from_image(finish(after_grad, grad, tok, w, small, experts))

    def add(*values):
        return functools.reduce(lambda a, b: a + b, [v.astype(F32) for v in values])

    if grouped:
        chips = add(grads[0], hop(grads[1], 1)).astype(BF)
        quarter = width // 4
        ways = [chips[a * quarter : (a + 1) * quarter] for a in range(4)]
        line = add(ways[0], *[hop(ways[a], 8 * a) for a in (1, 2, 3)]).astype(BF)
        line, tokens_grad, r_sent, g_in, g_out = after((line, tokens_grad, r_sent, g_in, g_out))
        step = width // 16
        cuts = [line[b * step : (b + 1) * step] for b in range(4)]
        chip = add(cuts[0], *[hop(cuts[b], 2 * b) for b in (1, 2, 3)])
        n_rows = step // 2
        keep = lax.dynamic_slice_in_dim(chip, core * n_rows, n_rows, 0)
        chip, block_out = after((chip, block_out))
        give = lax.dynamic_slice_in_dim(chip, (1 - core) * n_rows, n_rows, 0)
        got = hop(give.astype(BF), 1).astype(F32)
        dense = jnp.where(
            core == 0, jnp.concatenate([keep, got], axis=1), jnp.concatenate([got, keep], axis=1)
        )
    else:
        dense = lax.psum_scatter(grads[0], BOTH, scatter_dimension=0, tiled=True).astype(F32)
    side = dense[:, 4 * width :]
    vecs = [side[:, experts + k] for k in range(8)]
    return (
        block_out,
        tokens_grad,
        vecs[0],
        vecs[1],
        dense[:, : 3 * width],
        jnp.stack([vecs[5], vecs[7]], axis=0),
        dense[:, 3 * width : 4 * width],
        vecs[2],
        vecs[3],
        vecs[4],
        side[:, :experts],
        g_in,
        g_b_in,
        g_out,
        g_b_out,
    )


def solution(mesh):
    rows, line, cols = P(BOTH, None), P(BOTH), P(None, BOTH)
    experts = (P("expert", None, "dp"), P("expert", "dp"), P("expert", "dp", None), P("expert", "dp"))
    dense = (line, line, rows, cols, rows, line, line, line, rows)
    return jax.shard_map(
        functools.partial(local, (mesh.shape["dp"], mesh.shape["expert"])),
        mesh=mesh,
        in_specs=(rows, line, rows, P(), *dense, *experts, rows),
        out_specs=(rows, rows, *dense, *experts),
        check_vma=False,
    )
```

time: 1040 us -> 432 us (0.42)
  blocking collectives: 309 us -> 0 us
  matrix products: 257 us -> 42.3 us
  Pallas kernels: 0 us -> 167 us
  waiting for transfers between devices: 235 us -> 98.8 us
  other arithmetic: 122 us -> 19.2 us
  starting transfers between devices: 14.2 us -> 64.2 us
  local copies, waits for them, and re-layouts: 79 us -> 33.1 us
  between operations: 16.7 us -> 1.94 us
    dot_general x21 -> x9, matrix products: 257 us -> 42.3 us  [the longest x8 41.9 us: t_dot(): lax.dot_general(left, right, (((0,), (0,)), ((), ())), preferred_element_...]
    pallas_call x0 -> x10, Pallas kernels: none -> 167 us  [the longest x2 62.2 us: expert_call(): pl.pallas_call(functools.partial(expert_kernel, parts, len(before)), grid...]
    all_gather x3 -> x0, blocking collectives: 148 us -> none  [the longest x1 98.6 us: local(): lax.all_gather(router_weight, ('dp', 'expert'), axis=0, tiled=True)]
    reduce_scatter x4 -> x0, waiting for transfers between devices: 128 us -> none  [the longest x1 125 us: local(): lax.psum_scatter(qkv_weight_grad, ('dp', 'expert'), scatter_dimension=0,...]
    unnamed x3 -> x0, blocking collectives: 88 us -> none
    all_to_all x3 -> x6, waiting for transfers between devices: 104 us -> 24.5 us  [exchange(): return lax.all_to_all(blocks, 'expert', 0, 0, tiled=True)]
    ppermute x0 -> x37, waiting for transfers between devices: none -> 74.2 us  [hop(): return lax.ppermute(value, BOTH, [(i, i ^ mask) for i in range(devices)])]
    all_to_all x1 -> x0, blocking collectives: 73 us -> none  [local(): lax.all_to_all(slot_grad, 'expert', split_axis=0, concat_axis=0, tiled=True)]
  transfers between devices with their start and end apart: 13 -> 43, of which waited for: 4 -> 24; matrix products, arithmetic and copies ran while one was open for 37% -> 18% of each run, Pallas kernels for 0% -> 39%
where the time goes in v1:
time: 432 us; the launch traced here: 427 us
  Pallas kernels  167 us (39%)
  waiting for transfers between devices  98.8 us (23%)
  starting transfers between devices  64.2 us (15%)
  matrix products  42.3 us (10%)
  local copies, waits for them, and re-layouts  33.1 us (8%)
  other arithmetic  19.2 us (4%)
    ppermute x37, waiting for transfers between devices, hop(): return lax.ppermute(value, BOTH, [(i, i ^ mask) for i in range(devices)])  74.2 us
    pallas_call x2, Pallas kernels, expert_call(): pl.pallas_call(functools.partial(expert_kernel, parts, len(before)), grid...  62.2 us
    pallas_call x1, Pallas kernels, backward(): pl.pallas_call(functools.partial(backward_kernel, experts, n, split), gri...  45.1 us
    dot_general x8, matrix products, t_dot(): lax.dot_general(left, right, (((0,), (0,)), ((), ())), preferred_element_...  41.9 us
    ppermute x37, starting transfers between devices, hop(): return lax.ppermute(value, BOTH, [(i, i ^ mask) for i in range(devices)])  38.2 us
    all_to_all x6, starting transfers between devices, exchange(): return lax.all_to_all(blocks, 'expert', 0, 0, tiled=True)  26 us
    all_to_all x6, waiting for transfers between devices, exchange(): return lax.all_to_all(blocks, 'expert', 0, 0, tiled=True)  24.5 us
    pallas_call x1, Pallas kernels, forward(): pl.pallas_call(functools.partial(forward_kernel, experts, subs), grid=(im...  21 us
  transfers between devices with their start and end apart: 43, of which 24 were waited for; matrix products, arithmetic and copies ran while one was open for 18% of the time, Pallas kernels for 39%

profile of v1, /device:TPU:0, one launch (start us, length us, event | category | flops | bytes accessed | tf_op | source)
XLA Modules:
  0.0 426.9 jit_solution(10129056604649817450)
XLA Ops:
  0.7 1.4 copy.44.router
  2.8 3.4 concatenate.53
  6.9 1.8 pack_dense.1
  9.2 2.5 collective-permute-start.4
  11.7 1.5 collective-permute-start.5
  17.2 1.6 collective-permute-start.1
  18.8 2.6 collective-permute-start.2
  22.0 1.6 reshape.249
  26.5 6.4 %dispatch_plain.1 = bf16[8,2,128,768]{3,2,1,0:T(8,128)(2,1)} custom-call(s32[2,832]{1,0:T(2,128)} %pad_add_fusion.1.slots, bf16[832,768]{1,0:T(8,128)(2,1)} %bitcast.65), custom_call_target="tpu_custom_call" | custom-call | flops 1048576 | bytes 65536 | tf_op jit(solution)/shard_map/dispatch_plain/pallas_call | solution.py:243
  34.4 4.2 collective-permute-done.4.refs_5_
  38.6 1.5 collective-permute-done.5.refs_10_
  40.1 5.2 %all-to-all-start = ((bf16[8,2,128,768]{3,2,1,0:T(8,128)(2,1)}), bf16[8,2,128,768]{3,2,1,0:T(8,128)(2,1)S(1)}, u32[]{:S(2)}, u32[]{:S(2)}) async-start(bf16[8,2,128,768]{3,2,1,0:T(8,128)(2,1)} %dispatch_plain.1), calls=%async_computation | async-start | bytes 6291456 | tf_op jit(solution)/shard_map/all_to_all | solution.py:710
  45.9 1.5 collective-permute-start.7
  49.3 13.6 %collective-permute-done.6.refs_1_ = bf16[192,1664]{1,0:T(8,128)(2,1)} collective-permute-done((bf16[192,1664]{1,0:T(8,128)(2,1)}, bf16[192,1664]{1,0:T(8,128)(2,1)}, u32[]{:S(2)}, u32[]{:S(2)}) %collective-permute-start.6) | collective-permute-done | bytes 639008 | tf_op jit(solution)/shard_map/ppermute | solution.py:630
  62.9 12.6 %collective-permute-done.7.refs_2_ = bf16[192,1664]{1,0:T(8,128)(2,1)} collective-permute-done((bf16[192,1664]{1,0:T(8,128)(2,1)}, bf16[192,1664]{1,0:T(8,128)(2,1)}, u32[]{:S(2)}, u32[]{:S(2)}) %collective-permute-start.7) | collective-permute-done | bytes 639008 | tf_op jit(solution)/shard_map/ppermute | solution.py:630
  75.5 1.6 collective-permute-done.8.refs_3_
  77.9 1.5 collective-permute-start.14
  83.7 21.0 %tokens_forward.1 = (bf16[768,3328]{1,0:T(8,128)(2,1)}, f32[128,768]{1,0:T(8,128)}, bf16[4,208,2304]{2,1,0:T(8,128)(2,1)}, bf16[4,208,768]{2,1,0:T(8,128)(2,1)},...) custom-call(s32[40]{0:T(128)} %concatenate.52.off, ...), custom_call_target="tpu_custom_call" | custom-call | flops 1048576 | bytes 65536 | tf_op jit(solution)/shard_map/tokens_forward/pallas_call | solution.py:178
  105.3 5.3 %dispatch_a.1 = bf16[8,1,128,768]{3,2,1,0:T(8,128)(2,1)} custom-call(s32[2,832]{1,0:T(2,128)} %pad_add_fusion.1.slots, bf16[832,768]{1,0:T(8,128)(2,1)} %bitcast.63, f32[128,768]{1,0:T(8,128)} %get-tuple-element.88.refs_0_.small), custom_call_target="tpu_custom_call" | custom-call | flops 1048576 | bytes 65536 | tf_op jit(solution)/shard_map/dispatch_a/pallas_call | solution.py:243
  110.6 6.2 %all-to-all-done.refs_1_ = bf16[8,2,128,768]{3,2,1,0:T(8,128)(2,1)S(1)} async-done(((bf16[8,2,128,768]{3,2,1,0:T(8,128)(2,1)}), bf16[8,2,128,768]{3,2,1,0:T(8,128)(2,1)S(1)}, u32[]{:S(2)}, u32[]{:S(2)}) %all-to-all-start) | async-done | bytes 3145760 | tf_op jit(solution)/shard_map/all_to_all | solution.py:710
  116.8 4.3 %all-to-all-start.1 = ((bf16[8,1,128,768]{3,2,1,0:T(8,128)(2,1)}), bf16[8,1,128,768]{3,2,1,0:T(8,128)(2,1)}, u32[]{:S(2)}, u32[]{:S(2)}) async-start(bf16[8,1,128,768]{3,2,1,0:T(8,128)(2,1)} %dispatch_a.1), calls=%async_computation.1 | async-start | bytes 3145728 | tf_op jit(solution)/shard_map/all_to_all | solution.py:710
  121.1 1.6 collective-permute-start.15
  123.2 1.5 collective-permute-start.17
  125.2 1.5 collective-permute-start.19
  126.7 5.3 %dispatch_b.1 = bf16[8,1,128,768]{3,2,1,0:T(8,128)(2,1)} custom-call(s32[2,832]{1,0:T(2,128)} %pad_add_fusion.1.slots, bf16[832,768]{1,0:T(8,128)(2,1)} %bitcast.64, f32[128,768]{1,0:T(8,128)} %get-tuple-element.88.refs_0_.small), custom_call_target="tpu_custom_call" | custom-call | flops 1048576 | bytes 65536 | tf_op jit(solution)/shard_map/dispatch_b/pallas_call | solution.py:243
  132.0 19.2 %collective-permute-done.17 = bf16[8,768]{1,0:T(8,128)(2,1)S(1)} collective-permute-done((bf16[8,768]{1,0:T(8,128)(2,1)S(1)}, bf16[8,768]{1,0:T(8,128)(2,1)S(1)}, u32[]{:S(2)}, u32[]{:S(2)}) %collective-permute-start.17) | collective-permute-done | bytes 12320 | tf_op jit(solution)/shard_map/ppermute | solution.py:630
  151.3 7.7 %all-to-all-done.1.refs_0_ = bf16[8,1,128,768]{3,2,1,0:T(8,128)(2,1)} async-done(((bf16[8,1,128,768]{3,2,1,0:T(8,128)(2,1)}), bf16[8,1,128,768]{3,2,1,0:T(8,128)(2,1)}, u32[]{:S(2)}, u32[]{:S(2)}) %all-to-all-start.1) | async-done | bytes 1572896 | tf_op jit(solution)/shard_map/all_to_all | solution.py:710
  158.9 4.1 all-to-all-start.3
  163.7 30.8 %expert_a.1 = (bf16[2048,3072]{1,0:T(8,128)(2,1)}, bf16[2048,3072]{1,0:T(8,128)(2,1)}, bf16[2048,768]{1,0:T(8,128)(2,1)}, bf16[2048,768]{1,0:T(8,128)(2,1)}, bf1...) custom-call(bf16[8,1,128,768]{3,2,1,0:T(8,128)(2,1)} %all-to-all-done.1.r, ...), custom_call_target="tpu_custom_call" | custom-call | flops 1048576 | bytes 65536 | tf_op jit(solution)/shard_map/expert_a/pallas_call | solution.py:334
  194.6 6.2 %all-to-all-done.3.refs_0_ = bf16[8,1,128,768]{3,2,1,0:T(8,128)(2,1)S(1)} async-done(((bf16[8,1,128,768]{3,2,1,0:T(8,128)(2,1)}), bf16[8,1,128,768]{3,2,1,0:T(8,128)(2,1)S(1)}, u32[]{:S(2)}, u32[]{:S(2)}) %all-to-all-start.3) | async-done | bytes 1572896 | tf_op jit(solution)/shard_map/all_to_all | solution.py:710
  200.8 3.6 all-to-all-start.2
  206.3 31.4 %expert_b.1 = (bf16[2048,3072]{1,0:T(8,128)(2,1)}, bf16[2048,3072]{1,0:T(8,128)(2,1)}, bf16[2048,768]{1,0:T(8,128)(2,1)}, bf16[2048,768]{1,0:T(8,128)(2,1)}, bf1...) custom-call(bf16[8,1,128,768]{3,2,1,0:T(8,128)(2,1)} %copy-done.6, ...), custom_call_target="tpu_custom_call", output_to_operand_aliasing={{0}: (12, {}), {1}: (13, {}), {2}: (14, {}), {3}: (15, {}),... | custom-call | flops 1048576 | bytes 65536 | tf_op jit(solution)/shard_map/expert_b/pallas_call | solution.py:334
  237.7 4.5 %all-to-all-done.2.refs_0_ = bf16[8,128,768]{2,1,0:T(8,128)(2,1)S(1)} async-done(((bf16[8,128,768]{2,1,0:T(8,128)(2,1)}), bf16[8,128,768]{2,1,0:T(8,128)(2,1)S(1)}, u32[]{:S(2)}, u32[]{:S(2)}) %all-to-all-start.2) | async-done | bytes 1572896 | tf_op jit(solution)/shard_map/all_to_all | solution.py:710
  242.1 3.8 all-to-all-start.4
  245.9 5.8 %fusion.26 = bf16[768,768]{1,0:T(8,128)(2,1)S(1)} fusion(bf16[2048,768]{1,0:T(8,128)(2,1)} %get-tuple-element.117, bf16[2048,3072]{1,0:T(8,128)(2,1)} %get-tuple-element.116), kind=kOutput, calls=%fused_computation.26 | convolution fusion | flops 2416508928 | bytes 7471104 | tf_op jit(solution)/shard_map/dot_general | solution.py:35
  251.7 1.6 collective-permute-start.21
  253.3 5.6 %fusion.23 = bf16[768,768]{1,0:T(8,128)(2,1)S(1)} fusion(bf16[2048,768]{1,0:T(8,128)(2,1)} %get-tuple-element.114, bf16[2048,3072]{1,0:T(8,128)(2,1)} %get-tuple-element.115), kind=kOutput, calls=%fused_computation.25 | convolution fusion | flops 2416508928 | bytes 7471104 | tf_op jit(solution)/shard_map/dot_general | solution.py:35
  259.6 5.7 %fusion.20 = bf16[768,768]{1,0:T(8,128)(2,1)} fusion(bf16[2048,768]{1,0:T(8,128)(2,1)} %get-tuple-element.117, bf16[2048,3072]{1,0:T(8,128)(2,1)S(1)} %copy-done.2), kind=kOutput, calls=%fused_computation.24 | convolution fusion | flops 2416508928 | bytes 7471104 | tf_op jit(solution)/shard_map/dot_general | solution.py:35
  265.7 5.9 %fusion.17 = bf16[768,768]{1,0:T(8,128)(2,1)} fusion(bf16[2048,768]{1,0:T(8,128)(2,1)} %get-tuple-element.114, bf16[2048,3072]{1,0:T(8,128)(2,1)S(1)} %copy-done.3), kind=kOutput, calls=%fused_computation.23 | convolution fusion | flops 2416508928 | bytes 7471104 | tf_op jit(solution)/shard_map/dot_general | solution.py:35
  271.6 1.5 collective-permute-start.22
  273.1 7.5 %collective-permute-done.21 = bf16[768,768]{1,0:T(8,128)(2,1)S(1)} collective-permute-done((bf16[768,768]{1,0:T(8,128)(2,1)S(1)}, bf16[768,768]{1,0:T(8,128)(2,1)S(1)}, u32[]{:S(2)}, u32[]{:S(2)}) %collective-permute-start.21) | collective-permute-done | bytes 1179680 | tf_op jit(solution)/shard_map/ppermute | solution.py:630
  280.6 4.1 add_convert_fusion.1
  285.2 2.7 collective-permute-done.20
  287.8 3.8 add_convert_fusion.2
  292.1 4.2 fusion.8
  297.5 5.0 %all-to-all-start.5 = ((bf16[8,2,128,768]{3,2,1,0:T(8,128)(2,1)}), bf16[8,2,128,768]{3,2,1,0:T(8,128)(2,1)S(1)}, u32[]{:S(2)}, u32[]{:S(2)}) async-start(bf16[8,2,128,768]{3,2,1,0:T(8,128)(2,1)} %get-tuple-element.127), calls=%async_computation.5 | async-start | bytes 6291456 | tf_op jit(solution)/shard_map/all_to_all | solution.py:710
  302.5 7.0 %fusion.10 = f32[768,768]{1,0:T(8,128)} fusion(bf16[2048,768]{1,0:T(8,128)(2,1)} %get-tuple-element.114, bf16[2048,3072]{1,0:T(8,128)(2,1)} %get-tuple-element.115), kind=kOutput, calls=%fused_computation.11 | convolution fusion | flops 2415919104 | bytes 8650752 | tf_op jit(solution)/shard_map/dot_general | solution.py:35
  309.4 45.1 %tokens_backward.1 = (f32[4,208,768]{2,1,0:T(8,128)}, f32[4,208,128]{2,1,0:T(8,128)}, bf16[4,208,2304]{2,1,0:T(8,128)(2,1)}, bf16[768,1664]{1,0:T(8,128)(2,1)}, bf16[768,1664]{1,0:T(8,128)(2,1)}) custom-call(s32[18]{0:T(128)} %concatenate.50.off, s32[1]{0:T(128)} %copy.54.count, s32[4,208,2]{2,1,0:T(8,128)} %copy.45.slots, bf16[4,208,768]{2,1,0:T(8,128)(2,1)} %pad.12.cot, ...), custom_call_target="tpu_custom_call" | custom-call | flops 1048576 | bytes 65536 | tf_op jit(solution)/shard_map/tokens_backward/pallas_call | solution.py:508
  356.6 1.5 collective-permute-start.35
  360.3 2.4 collective-permute-done.36
  362.8 3.1 add_convert_fusion
  367.2 1.5 collective-permute-start.27
  369.2 1.5 collective-permute-start.29
  370.7 3.4 add_bitcast_fusion
  374.2 3.4 add_bitcast_fusion.1
  377.6 10.1 %tokens_finish.1 = f32[4,208,768]{2,1,0:T(8,128)} custom-call(f32[4,208,768]{2,1,0:T(8,128)} %get-tuple-element.124.after_grad, bf16[4,208,2304]{2,1,0:T(8,128)(2,1)} %get-tuple-element.125.grad, bf16[4,208,768]{2,1,0:T(8,128)(2,1)} %pad.13.tok, bf16[768,3328]{1,0:T(8,128)(2,1)} %get-tuple-element.87.w, f32[128,768]{1,0:T(8,128)} %get-tuple-element.88.refs_0_.small), custom_call_target="tpu_custom_call" | custom-call | flops 1048576 | bytes 65536 | tf_op jit(solution)/shard_map/tokens_finish/pallas_call | solution.py:544
  387.7 3.3 slice.187
  391.0 3.4 reshape.257
  394.4 2.7 collective-permute-done.28
  397.1 2.8 add_convert_fusion.3
  399.9 2.4 fusion.58
  402.2 2.0 collective-permute-start.30
  404.2 2.4 collective-permute-start.31
  407.9 10.3 %block_output.1 = bf16[4,208,768]{2,1,0:T(8,128)(2,1)} custom-call(s32[1]{0:T(128)} %copy.54.count, s32[4,208,2]{2,1,0:T(8,128)} %copy.45.slots, f32[4,208,768]{2,1,0:T(8,128)} %get-tuple-element.84.aa, f32[4,208,128]{2,1,0:T(8,128)} %get-tuple-element.129.probs, bf16[8,2,128,768]{3,2,1,0:T(8,128)(2,1)} %copy-done.1), custom_call_target="tpu_custom_call" | custom-call | flops 1048576 | bytes 65536 | tf_op jit(solution)/shard_map/block_output/pallas_call | solution.py:579
  (149 shorter events, 41.1 us)
Async XLA Ops:
  0.6 21.0 %copy-start.12 = (bf16[788,768]{1,0:T(8,128)(2,1)S(1)}, bf16[788,768]{1,0:T(8,128)(2,1)}, u32[]{:S(2)}) copy-start(bf16[788,768]{1,0:T(8,128)(2,1)} %param.18) | copy-start | bytes 3631108
  8.7 7.4 %collective-permute-start = (bf16[24,1664]{1,0:T(8,128)(2,1)}, bf16[24,1664]{1,0:T(8,128)(2,1)S(1)}, u32[]{:S(2)}, u32[]{:S(2)}) collective-permute-start(bf16[24,1664]{1,0:T(8,128)(2,1)} %get-tuple-element.78), channel_id=1, source_target_pairs={{0,1},{1,0},{2,3},{3,2},{4,5},{5,4},{6,7},{7,6},{8,9},{9,8},{10,11... | collective-permute-start | bytes 239624 | tf_op jit(solution)/shard_map/ppermute | solution.py:630
  9.2 29.4 %collective-permute-start.4 = (bf16[768,768]{1,0:T(8,128)(2,1)}, bf16[768,768]{1,0:T(8,128)(2,1)}, u32[]{:S(2)}, u32[]{:S(2)}) collective-permute-start(bf16[768,768]{1,0:T(8,128)(2,1)} %bitcast.66), channel_id=1, source_target_pairs={{0,8},{1,9},{2,10},{3,11},{4,12},{5,13},{6,14},{7,15},{8,0},{9,1},... | collective-permute-start | bytes 3538952 | tf_op jit(solution)/shard_map/ppermute | solution.py:630
  11.7 28.4 %collective-permute-start.5 = (bf16[768,768]{1,0:T(8,128)(2,1)}, bf16[768,768]{1,0:T(8,128)(2,1)}, u32[]{:S(2)}, u32[]{:S(2)}) collective-permute-start(bf16[768,768]{1,0:T(8,128)(2,1)} %bitcast.70), channel_id=1, source_target_pairs={{0,16},{1,17},{2,18},{3,19},{4,20},{5,21},{6,22},{7,23},{8,24},{9,... | collective-permute-start | bytes 3538952 | tf_op jit(solution)/shard_map/ppermute | solution.py:630
  17.2 15.7 %collective-permute-start.1 = (bf16[48,1664]{1,0:T(8,128)(2,1)S(1)}, bf16[48,1664]{1,0:T(8,128)(2,1)S(1)}, u32[]{:S(2)}, u32[]{:S(2)}) collective-permute-start(bf16[48,1664]{1,0:T(8,128)(2,1)S(1)} %maximum_select_fusion.1), channel_id=1, source_target_pairs={{0,2},{1,3},{2,0},{3,1},{4,6},{5,7},{6,4},{7,5},{8,10},{9,11},{10,... | collective-permute-start | bytes 479240 | tf_op jit(solution)/shard_map/ppermute | solution.py:630
  18.8 14.8 %collective-permute-start.2 = (bf16[48,1664]{1,0:T(8,128)(2,1)S(1)}, bf16[48,1664]{1,0:T(8,128)(2,1)S(1)}, u32[]{:S(2)}, u32[]{:S(2)}) collective-permute-start(bf16[48,1664]{1,0:T(8,128)(2,1)S(1)} %maximum_select_fusion.1), channel_id=1, source_target_pairs={{0,4},{1,5},{2,6},{3,7},{4,0},{5,1},{6,2},{7,3},{8,12},{9,13},{10,... | collective-permute-start | bytes 479240 | tf_op jit(solution)/shard_map/ppermute | solution.py:630
  21.4 12.2 %collective-permute-start.3 = (bf16[48,1664]{1,0:T(8,128)(2,1)S(1)}, bf16[48,1664]{1,0:T(8,128)(2,1)S(1)}, u32[]{:S(2)}, u32[]{:S(2)}) collective-permute-start(bf16[48,1664]{1,0:T(8,128)(2,1)S(1)} %maximum_select_fusion.1), channel_id=1, source_target_pairs={{0,6},{1,7},{2,4},{3,5},{4,2},{5,3},{6,0},{7,1},{8,14},{9,15},{10,... | collective-permute-start | bytes 479240 | tf_op jit(solution)/shard_map/ppermute | solution.py:630
  34.4 14.5 %copy-start.17 = (bf16[1,192]{1,0:T(2,128)(2,1)S(1)}, bf16[1,192]{1,0:T(2,128)(2,1)}, u32[]{:S(2)}) copy-start(bf16[1,192]{1,0:T(2,128)(2,1)} %param.34) | copy-start | bytes 1156
  34.4 14.7 %copy-start.16 = (bf16[1,768]{1,0:T(2,128)(2,1)S(1)}, bf16[1,768]{1,0:T(2,128)(2,1)}, u32[]{:S(2)}) copy-start(bf16[1,768]{1,0:T(2,128)(2,1)} %param.32) | copy-start | bytes 4612
  40.1 76.7 %all-to-all-start = ((bf16[8,2,128,768]{3,2,1,0:T(8,128)(2,1)}), bf16[8,2,128,768]{3,2,1,0:T(8,128)(2,1)S(1)}, u32[]{:S(2)}, u32[]{:S(2)}) async-start(bf16[8,2,128,768]{3,2,1,0:T(8,128)(2,1)} %dispatch_plain.1), calls=%async_computation | async-start | bytes 6291456 | tf_op jit(solution)/shard_map/all_to_all | solution.py:710
  45.3 17.6 %collective-permute-start.6 = (bf16[192,1664]{1,0:T(8,128)(2,1)}, bf16[192,1664]{1,0:T(8,128)(2,1)}, u32[]{:S(2)}, u32[]{:S(2)}) collective-permute-start(bf16[192,1664]{1,0:T(8,128)(2,1)} %pad_maximum_fusion.refs_0_), channel_id=1, source_target_pairs={{0,8},{1,9},{2,10},{3,11},{4,12},{5,13},{6,14},{7,15},{8,0},{9,1},... | collective-permute-start | bytes 1916936 | tf_op jit(solution)/shard_map/ppermute | solution.py:630
  45.9 29.6 %collective-permute-start.7 = (bf16[192,1664]{1,0:T(8,128)(2,1)}, bf16[192,1664]{1,0:T(8,128)(2,1)}, u32[]{:S(2)}, u32[]{:S(2)}) collective-permute-start(bf16[192,1664]{1,0:T(8,128)(2,1)} %pad_maximum_fusion.refs_0_), channel_id=1, source_target_pairs={{0,16},{1,17},{2,18},{3,19},{4,20},{5,21},{6,22},{7,23},{8,24},{9,... | collective-permute-start | bytes 1916936 | tf_op jit(solution)/shard_map/ppermute | solution.py:630
  47.4 29.7 %collective-permute-start.8 = (bf16[192,1664]{1,0:T(8,128)(2,1)}, bf16[192,1664]{1,0:T(8,128)(2,1)}, u32[]{:S(2)}, u32[]{:S(2)}) collective-permute-start(bf16[192,1664]{1,0:T(8,128)(2,1)} %pad_maximum_fusion.refs_0_), channel_id=1, source_target_pairs={{0,24},{1,25},{2,26},{3,27},{4,28},{5,29},{6,30},{7,31},{8,16},{9,... | collective-permute-start | bytes 1916936 | tf_op jit(solution)/shard_map/ppermute | solution.py:630
  49.1 30.9 %collective-permute-start.9 = (bf16[192,1664]{1,0:T(8,128)(2,1)}, bf16[192,1664]{1,0:T(8,128)(2,1)}, u32[]{:S(2)}, u32[]{:S(2)}) collective-permute-start(bf16[192,1664]{1,0:T(8,128)(2,1)} %pad_maximum_fusion.refs_0_), channel_id=1, source_target_pairs={{0,1},{1,0},{2,3},{3,2},{4,5},{5,4},{6,7},{7,6},{8,9},{9,8},{10,11... | collective-permute-start | bytes 1916936 | tf_op jit(solution)/shard_map/ppermute | solution.py:630
  77.1 27.9 %collective-permute-start.13 = (bf16[768,768]{1,0:T(8,128)(2,1)}, bf16[768,768]{1,0:T(8,128)(2,1)}, u32[]{:S(2)}, u32[]{:S(2)}) collective-permute-start(bf16[768,768]{1,0:T(8,128)(2,1)} %bitcast.67), channel_id=1, source_target_pairs={{0,16},{1,17},{2,18},{3,19},{4,20},{5,21},{6,22},{7,23},{8,24},{9,... | collective-permute-start | bytes 3538952 | tf_op jit(solution)/shard_map/ppermute | solution.py:630
  77.9 27.4 %collective-permute-start.14 = (bf16[768,768]{1,0:T(8,128)(2,1)}, bf16[768,768]{1,0:T(8,128)(2,1)}, u32[]{:S(2)}, u32[]{:S(2)}) collective-permute-start(bf16[768,768]{1,0:T(8,128)(2,1)} %bitcast.71), channel_id=1, source_target_pairs={{0,8},{1,9},{2,10},{3,11},{4,12},{5,13},{6,14},{7,15},{8,0},{9,1},... | collective-permute-start | bytes 3538952 | tf_op jit(solution)/shard_map/ppermute | solution.py:630
  79.4 2.4 collective-permute-start.10
  79.4 3.3 collective-permute-start.11
  79.9 3.7 collective-permute-start.12
  116.8 15.2 %copy-start = (bf16[8,2,128,768]{3,2,1,0:T(8,128)(2,1)}, bf16[8,2,128,768]{3,2,1,0:T(8,128)(2,1)S(1)}, u32[]{:S(2)}) copy-start(bf16[8,2,128,768]{3,2,1,0:T(8,128)(2,1)S(1)} %all-to-all-done.refs_1_) | copy-start | bytes 9437188
  116.8 42.2 %all-to-all-start.1 = ((bf16[8,1,128,768]{3,2,1,0:T(8,128)(2,1)}), bf16[8,1,128,768]{3,2,1,0:T(8,128)(2,1)}, u32[]{:S(2)}, u32[]{:S(2)}) async-start(bf16[8,1,128,768]{3,2,1,0:T(8,128)(2,1)} %dispatch_a.1), calls=%async_computation.1 | async-start | bytes 3145728 | tf_op jit(solution)/shard_map/all_to_all | solution.py:710
  121.1 30.2 %collective-permute-start.15 = (bf16[768,768]{1,0:T(8,128)(2,1)}, bf16[768,768]{1,0:T(8,128)(2,1)}, u32[]{:S(2)}, u32[]{:S(2)}) collective-permute-start(bf16[768,768]{1,0:T(8,128)(2,1)} %collective-permute-done.4.refs_5_), channel_id=1, source_target_pairs={{0,16},{1,17},{2,18},{3,19},{4,20},{5,21},{6,22},{7,23},{8,24},{9,... | collective-permute-start | bytes 3538952 | tf_op jit(solution)/shard_map/ppermute | solution.py:630
  122.7 28.6 %collective-permute-start.16 = (bf16[768,768]{1,0:T(8,128)(2,1)}, bf16[768,768]{1,0:T(8,128)(2,1)}, u32[]{:S(2)}, u32[]{:S(2)}) collective-permute-start(bf16[768,768]{1,0:T(8,128)(2,1)} %collective-permute-done.5.refs_10_), channel_id=1, source_target_pairs={{0,8},{1,9},{2,10},{3,11},{4,12},{5,13},{6,14},{7,15},{8,0},{9,1},... | collective-permute-start | bytes 3538952 | tf_op jit(solution)/shard_map/ppermute | solution.py:630
  123.2 28.0 %collective-permute-start.17 = (bf16[8,768]{1,0:T(8,128)(2,1)S(1)}, bf16[8,768]{1,0:T(8,128)(2,1)S(1)}, u32[]{:S(2)}, u32[]{:S(2)}) collective-permute-start(bf16[8,768]{1,0:T(8,128)(2,1)S(1)} %maximum_maximum_fusion), channel_id=1, source_target_pairs={{0,8},{1,9},{2,10},{3,11},{4,12},{5,13},{6,14},{7,15},{8,0},{9,1},... | collective-permute-start | bytes 36872 | tf_op jit(solution)/shard_map/ppermute | solution.py:630
  124.7 26.5 %collective-permute-start.18 = (bf16[8,768]{1,0:T(8,128)(2,1)S(1)}, bf16[8,768]{1,0:T(8,128)(2,1)S(1)}, u32[]{:S(2)}, u32[]{:S(2)}) collective-permute-start(bf16[8,768]{1,0:T(8,128)(2,1)S(1)} %maximum_maximum_fusion), channel_id=1, source_target_pairs={{0,16},{1,17},{2,18},{3,19},{4,20},{5,21},{6,22},{7,23},{8,24},{9,... | collective-permute-start | bytes 36872 | tf_op jit(solution)/shard_map/ppermute | solution.py:630
  125.2 26.1 %collective-permute-start.19 = (bf16[8,768]{1,0:T(8,128)(2,1)S(1)}, bf16[8,768]{1,0:T(8,128)(2,1)S(1)}, u32[]{:S(2)}, u32[]{:S(2)}) collective-permute-start(bf16[8,768]{1,0:T(8,128)(2,1)S(1)} %maximum_maximum_fusion), channel_id=1, source_target_pairs={{0,24},{1,25},{2,26},{3,27},{4,28},{5,29},{6,30},{7,31},{8,16},{9,... | collective-permute-start | bytes 36872 | tf_op jit(solution)/shard_map/ppermute | solution.py:630
  158.9 41.9 %all-to-all-start.3 = ((bf16[8,1,128,768]{3,2,1,0:T(8,128)(2,1)}), bf16[8,1,128,768]{3,2,1,0:T(8,128)(2,1)S(1)}, u32[]{:S(2)}, u32[]{:S(2)}) async-start(bf16[8,1,128,768]{3,2,1,0:T(8,128)(2,1)} %dispatch_b.1), calls=%async_computation.3 | async-start | bytes 3145728 | tf_op jit(solution)/shard_map/all_to_all | solution.py:710
  163.1 0.7 copy-start.13
  200.8 5.5 %copy-start.6 = (bf16[8,1,128,768]{3,2,1,0:T(8,128)(2,1)}, bf16[8,1,128,768]{3,2,1,0:T(8,128)(2,1)S(1)}, u32[]{:S(2)}) copy-start(bf16[8,1,128,768]{3,2,1,0:T(8,128)(2,1)S(1)} %all-to-all-done.3.refs_0_) | copy-start | bytes 4718596
  200.8 41.3 %all-to-all-start.2 = ((bf16[8,128,768]{2,1,0:T(8,128)(2,1)}), bf16[8,128,768]{2,1,0:T(8,128)(2,1)S(1)}, u32[]{:S(2)}, u32[]{:S(2)}) async-start(bf16[8,128,768]{2,1,0:T(8,128)(2,1)} %get-tuple-element.101), calls=%async_computation.2 | async-start | bytes 3145728 | tf_op jit(solution)/shard_map/all_to_all | solution.py:710
  242.1 9.5 %copy-start.5 = (bf16[8,128,768]{2,1,0:T(8,128)(2,1)}, bf16[8,128,768]{2,1,0:T(8,128)(2,1)S(1)}, u32[]{:S(2)}) copy-start(bf16[8,128,768]{2,1,0:T(8,128)(2,1)S(1)} %all-to-all-done.2.refs_0_) | copy-start | bytes 4718596
  242.1 54.2 %all-to-all-start.4 = ((bf16[8,128,768]{2,1,0:T(8,128)(2,1)}), bf16[8,128,768]{2,1,0:T(8,128)(2,1)S(1)}, u32[]{:S(2)}, u32[]{:S(2)}) async-start(bf16[8,128,768]{2,1,0:T(8,128)(2,1)} %get-tuple-element.109), calls=%async_computation.4 | async-start | bytes 3145728 | tf_op jit(solution)/shard_map/all_to_all | solution.py:710
  245.9 13.7 %copy-start.2 = (bf16[2048,3072]{1,0:T(8,128)(2,1)S(1)}, bf16[2048,3072]{1,0:T(8,128)(2,1)}, u32[]{:S(2)}) copy-start(bf16[2048,3072]{1,0:T(8,128)(2,1)} %get-tuple-element.116) | copy-start | bytes 37748740
  251.7 28.9 %collective-permute-start.21 = (bf16[768,768]{1,0:T(8,128)(2,1)S(1)}, bf16[768,768]{1,0:T(8,128)(2,1)S(1)}, u32[]{:S(2)}, u32[]{:S(2)}) collective-permute-start(bf16[768,768]{1,0:T(8,128)(2,1)S(1)} %fusion.26), channel_id=1, source_target_pairs={{0,16},{1,17},{2,18},{3,19},{4,20},{5,21},{6,22},{7,23},{8,24},{9,... | collective-permute-start | bytes 3538952 | tf_op jit(solution)/shard_map/ppermute | solution.py:630
  253.3 12.5 %copy-start.3 = (bf16[2048,3072]{1,0:T(8,128)(2,1)S(1)}, bf16[2048,3072]{1,0:T(8,128)(2,1)}, u32[]{:S(2)}) copy-start(bf16[2048,3072]{1,0:T(8,128)(2,1)} %get-tuple-element.115) | copy-start | bytes 37748740
  258.9 28.9 %collective-permute-start.20 = (bf16[768,768]{1,0:T(8,128)(2,1)S(1)}, bf16[768,768]{1,0:T(8,128)(2,1)S(1)}, u32[]{:S(2)}, u32[]{:S(2)}) collective-permute-start(bf16[768,768]{1,0:T(8,128)(2,1)S(1)} %fusion.23), channel_id=1, source_target_pairs={{0,8},{1,9},{2,10},{3,11},{4,12},{5,13},{6,14},{7,15},{8,0},{9,1},... | collective-permute-start | bytes 3538952 | tf_op jit(solution)/shard_map/ppermute | solution.py:630
  265.2 15.3 %copy-start.9 = (bf16[2048,768]{1,0:T(8,128)(2,1)S(1)}, bf16[2048,768]{1,0:T(8,128)(2,1)}, u32[]{:S(2)}) copy-start(bf16[2048,768]{1,0:T(8,128)(2,1)} %get-tuple-element.117) | copy-start | bytes 9437188
  265.2 89.3 %collective-permute-start.23 = (bf16[768,768]{1,0:T(8,128)(2,1)}, bf16[768,768]{1,0:T(8,128)(2,1)}, u32[]{:S(2)}, u32[]{:S(2)}) collective-permute-start(bf16[768,768]{1,0:T(8,128)(2,1)} %fusion.20), channel_id=1, source_target_pairs={{0,16},{1,17},{2,18},{3,19},{4,20},{5,21},{6,22},{7,23},{8,24},{9,... | collective-permute-start | bytes 3538952 | tf_op jit(solution)/shard_map/ppermute | solution.py:630
  271.6 16.2 %copy-start.8 = (bf16[2048,768]{1,0:T(8,128)(2,1)S(1)}, bf16[2048,768]{1,0:T(8,128)(2,1)}, u32[]{:S(2)}) copy-start(bf16[2048,768]{1,0:T(8,128)(2,1)} %get-tuple-element.114) | copy-start | bytes 9437188
  271.6 83.0 %collective-permute-start.22 = (bf16[768,768]{1,0:T(8,128)(2,1)}, bf16[768,768]{1,0:T(8,128)(2,1)}, u32[]{:S(2)}, u32[]{:S(2)}) collective-permute-start(bf16[768,768]{1,0:T(8,128)(2,1)} %fusion.17), channel_id=1, source_target_pairs={{0,8},{1,9},{2,10},{3,11},{4,12},{5,13},{6,14},{7,15},{8,0},{9,1},... | collective-permute-start | bytes 3538952 | tf_op jit(solution)/shard_map/ppermute | solution.py:630
  284.6 70.0 %collective-permute-start.25 = (bf16[768,768]{1,0:T(8,128)(2,1)}, bf16[768,768]{1,0:T(8,128)(2,1)}, u32[]{:S(2)}, u32[]{:S(2)}) collective-permute-start(bf16[768,768]{1,0:T(8,128)(2,1)} %add_convert_fusion.1), channel_id=1, source_target_pairs={{0,8},{1,9},{2,10},{3,11},{4,12},{5,13},{6,14},{7,15},{8,0},{9,1},... | collective-permute-start | bytes 3538952 | tf_op jit(solution)/shard_map/ppermute | solution.py:630
  291.6 63.0 %collective-permute-start.24 = (bf16[768,768]{1,0:T(8,128)(2,1)}, bf16[768,768]{1,0:T(8,128)(2,1)}, u32[]{:S(2)}, u32[]{:S(2)}) collective-permute-start(bf16[768,768]{1,0:T(8,128)(2,1)} %add_convert_fusion.2), channel_id=1, source_target_pairs={{0,16},{1,17},{2,18},{3,19},{4,20},{5,21},{6,22},{7,23},{8,24},{9,... | collective-permute-start | bytes 3538952 | tf_op jit(solution)/shard_map/ppermute | solution.py:630
  296.3 1.1 copy-start.7
  297.5 102.4 %all-to-all-start.5 = ((bf16[8,2,128,768]{3,2,1,0:T(8,128)(2,1)}), bf16[8,2,128,768]{3,2,1,0:T(8,128)(2,1)S(1)}, u32[]{:S(2)}, u32[]{:S(2)}) async-start(bf16[8,2,128,768]{3,2,1,0:T(8,128)(2,1)} %get-tuple-element.127), calls=%async_computation.5 | async-start | bytes 6291456 | tf_op jit(solution)/shard_map/all_to_all | solution.py:710
  309.4 45.8 %copy-start.14 = (f32[4,8,768]{2,1,0:T(8,128)S(1)}, f32[4,8,768]{2,1,0:T(8,128)}, u32[]{:S(2)}) copy-start(f32[4,8,768]{2,1,0:T(8,128)} %get-tuple-element.134) | copy-start | bytes 294916
  309.4 45.8 %copy-start.15 = (f32[4,8,768]{2,1,0:T(8,128)S(1)}, f32[4,8,768]{2,1,0:T(8,128)}, u32[]{:S(2)}) copy-start(f32[4,8,768]{2,1,0:T(8,128)} %get-tuple-element.135) | copy-start | bytes 294916
  354.6 8.2 %collective-permute-start.26 = (bf16[768,1664]{1,0:T(8,128)(2,1)}, bf16[768,1664]{1,0:T(8,128)(2,1)}, u32[]{:S(2)}, u32[]{:S(2)}) collective-permute-start(bf16[768,1664]{1,0:T(8,128)(2,1)} %get-tuple-element.123), channel_id=1, source_target_pairs={{0,1},{1,0},{2,3},{3,2},{4,5},{5,4},{6,7},{7,6},{8,9},{9,8},{10,11... | collective-permute-start | bytes 7667720 | tf_op jit(solution)/shard_map/ppermute | solution.py:630
  356.1 3.7 collective-permute-start.34
  356.6 3.7 collective-permute-start.35
  358.1 4.6 %collective-permute-start.36 = (bf16[8,768]{1,0:T(8,128)(2,1)S(1)}, bf16[8,768]{1,0:T(8,128)(2,1)S(1)}, u32[]{:S(2)}, u32[]{:S(2)}) collective-permute-start(bf16[8,768]{1,0:T(8,128)(2,1)S(1)} %get-tuple-element.215), channel_id=1, source_target_pairs={{0,24},{1,25},{2,26},{3,27},{4,28},{5,29},{6,30},{7,31},{8,16},{9,... | collective-permute-start | bytes 36872 | tf_op jit(solution)/shard_map/ppermute | solution.py:630
  365.9 8.3 %copy-start.4 = (bf16[768,1664]{1,0:T(8,128)(2,1)}, bf16[768,1664]{1,0:T(8,128)(2,1)S(1)}, u32[]{:S(2)}) copy-start(bf16[768,1664]{1,0:T(8,128)(2,1)S(1)} %add_convert_fusion) | copy-start | bytes 7667716
  365.9 4.8 %copy-start.10 = (f32[768,768]{1,0:T(8,128)S(1)}, f32[768,768]{1,0:T(8,128)}, u32[]{:S(2)}) copy-start(f32[768,768]{1,0:T(8,128)} %fusion.8) | copy-start | bytes 7077892
  367.2 27.1 %collective-permute-start.27 = (bf16[192,1664]{1,0:T(8,128)(2,1)}, bf16[192,1664]{1,0:T(8,128)(2,1)}, u32[]{:S(2)}, u32[]{:S(2)}) collective-permute-start(bf16[192,1664]{1,0:T(8,128)(2,1)} %get-tuple-element.199), channel_id=1, source_target_pairs={{0,8},{1,9},{2,10},{3,11},{4,12},{5,13},{6,14},{7,15},{8,0},{9,1},... | collective-permute-start | bytes 1916936 | tf_op jit(solution)/shard_map/ppermute | solution.py:630
  368.7 28.3 %collective-permute-start.28 = (bf16[192,1664]{1,0:T(8,128)(2,1)}, bf16[192,1664]{1,0:T(8,128)(2,1)}, u32[]{:S(2)}, u32[]{:S(2)}) collective-permute-start(bf16[192,1664]{1,0:T(8,128)(2,1)} %get-tuple-element.201), channel_id=1, source_target_pairs={{0,16},{1,17},{2,18},{3,19},{4,20},{5,21},{6,22},{7,23},{8,24},{9,... | collective-permute-start | bytes 1916936 | tf_op jit(solution)/shard_map/ppermute | solution.py:630
  369.2 4.9 %copy-start.11 = (f32[768,768]{1,0:T(8,128)S(1)}, f32[768,768]{1,0:T(8,128)}, u32[]{:S(2)}) copy-start(f32[768,768]{1,0:T(8,128)} %fusion.10) | copy-start | bytes 7077892
  369.2 27.8 %collective-permute-start.29 = (bf16[192,1664]{1,0:T(8,128)(2,1)}, bf16[192,1664]{1,0:T(8,128)(2,1)}, u32[]{:S(2)}, u32[]{:S(2)}) collective-permute-start(bf16[192,1664]{1,0:T(8,128)(2,1)} %get-tuple-element.200), channel_id=1, source_target_pairs={{0,24},{1,25},{2,26},{3,27},{4,28},{5,29},{6,30},{7,31},{8,16},{9,... | collective-permute-start | bytes 1916936 | tf_op jit(solution)/shard_map/ppermute | solution.py:630
  399.9 8.0 %copy-start.1 = (bf16[8,2,128,768]{3,2,1,0:T(8,128)(2,1)}, bf16[8,2,128,768]{3,2,1,0:T(8,128)(2,1)S(1)}, u32[]{:S(2)}) copy-start(bf16[8,2,128,768]{3,2,1,0:T(8,128)(2,1)S(1)} %all-to-all-done.5.outs) | copy-start | bytes 9437188
  402.2 18.5 %collective-permute-start.30 = (bf16[48,1664]{1,0:T(8,128)(2,1)}, bf16[48,1664]{1,0:T(8,128)(2,1)S(1)}, u32[]{:S(2)}, u32[]{:S(2)}) collective-permute-start(bf16[48,1664]{1,0:T(8,128)(2,1)} %get-tuple-element.202), channel_id=1, source_target_pairs={{0,2},{1,3},{2,0},{3,1},{4,6},{5,7},{6,4},{7,5},{8,10},{9,11},{10,... | collective-permute-start | bytes 479240 | tf_op jit(solution)/shard_map/ppermute | solution.py:630
  404.2 16.5 %collective-permute-start.31 = (bf16[48,1664]{1,0:T(8,128)(2,1)}, bf16[48,1664]{1,0:T(8,128)(2,1)}, u32[]{:S(2)}, u32[]{:S(2)}) collective-permute-start(bf16[48,1664]{1,0:T(8,128)(2,1)} %get-tuple-element.204), channel_id=1, source_target_pairs={{0,4},{1,5},{2,6},{3,7},{4,0},{5,1},{6,2},{7,3},{8,12},{9,13},{10,... | collective-permute-start | bytes 479240 | tf_op jit(solution)/shard_map/ppermute | solution.py:630
  406.6 14.2 %collective-permute-start.32 = (bf16[48,1664]{1,0:T(8,128)(2,1)S(1)}, bf16[48,1664]{1,0:T(8,128)(2,1)}, u32[]{:S(2)}, u32[]{:S(2)}) collective-permute-start(bf16[48,1664]{1,0:T(8,128)(2,1)S(1)} %get-tuple-element.203), channel_id=1, source_target_pairs={{0,6},{1,7},{2,4},{3,5},{4,2},{5,3},{6,0},{7,1},{8,14},{9,15},{10,... | collective-permute-start | bytes 479240 | tf_op jit(solution)/shard_map/ppermute | solution.py:630
  418.1 1.3 slice-start
  421.9 1.3 collective-permute-start.33
